TPU v7x, 512 devices: a whole 4x8x8 slice. The times are simulated.
512 devices in a mesh: row: 32 (over x_lo, z, core), col: 16 (over x_hi, y).
Axes of the slice: x: 4 (x_hi: 2, x_lo: 2; x = x_hi * 2 + x_lo), y: 8, z: 8, core: 2. Of those that a mesh axis runs over, the one named last changes fastest.
Arguments:
- features: bfloat16 [65536, 128], P(('row', 'col')), may hold values from -6 to 6
- degrees: int32 [65536], P(('row', 'col')), may hold values from 16 to 256
- proj_weight: bfloat16 [128, 512], replicated, may hold values from -0.5 to 0.5
- bias: float32 [512], replicated, may hold values from -3 to 3
- grad_out: bfloat16 [65536, 512], P(('row', 'col')), may hold values from -6 to 6
- tile_slots: int32 [32, 16, 32, 2], P('row', 'col'), may hold values from -1 to 31, as said below
- tile_values: bfloat16 [32, 16, 32, 128, 128], P('row', 'col'), may hold values from -4 to 4
Outputs:
- activations: bfloat16 [65536, 512], P(('row', 'col'))
- grad_weight: float32 [128, 512], replicated
- grad_bias: float32 [512], replicated
- grad_features: bfloat16 [65536, 128], P(('row', 'col'))
Inputs may be any that keep to these rules, and one draw needn't show every extreme that they name: `tile_slots`: entry [r, c, k] gives slot k's tile row (below 16) and tile column (below 32) in grid cell (r, c)'s block, both -1 for an empty slot. Live slots come first, hold distinct positions and stand in ascending order of tile column. Every grid cell has at least 4 live slots, and one grid cell has all 32 live.
All inputs are finite; a program needn't handle non-finite values.
Results may differ from a plain program's by a relative error of at most 0.0062.
Values may be sent and summed in bfloat16 or wider, within the bound.
A program may use at most 64 MiB of HBM per device.

v0:
```python
import math

import jax
import jax.numpy as jnp
from jax import lax
from jax.sharding import PartitionSpec as P


def gelu_tanh(values):
    return jax.nn.gelu(values, approximate=True)


def slot_turns(slots, group):
    return slots.shape[0] // group


def aggregate(columns, values, slots, block_rows):
    tile_size = values.shape[1]
    width = columns.shape[1]
    row_tiles = block_rows // tile_size
    stacked = columns.reshape(-1, tile_size, width)
    group = math.gcd(slots.shape[0], 8)

    def turn(group_index, totals):
        first = group_index * group
        tiles = lax.dynamic_slice_in_dim(values, first, group, 0)
        places = lax.dynamic_slice_in_dim(slots, first, group, 0)
        active = places[:, 0] >= 0
        tile_rows = jnp.maximum(places[:, 0], 0)
        tile_cols = jnp.maximum(places[:, 1], 0)
        picked = stacked[tile_cols]
        products = jnp.einsum("gij,gjf->gif", tiles, picked, preferred_element_type=jnp.float32)
        products = jnp.where(active[:, None, None], products, jnp.float32(0.0))
        return totals.at[tile_rows].add(products)

    start = jnp.zeros((row_tiles, tile_size, width), jnp.float32)
    totals = lax.fori_loop(0, slot_turns(slots, group), turn, start)
    return totals.reshape(block_rows, width)


def aggregate_back(rows_in, values, slots, out_rows, first_row, row_count):
    tile_size = values.shape[1]
    width = rows_in.shape[1]
    col_tiles = out_rows // tile_size
    stacked = rows_in.reshape(-1, tile_size, width)
    group = math.gcd(slots.shape[0], 8)

    def turn(group_index, totals):
        first = group_index * group
        tiles = lax.dynamic_slice_in_dim(values, first, group, 0)
        places = lax.dynamic_slice_in_dim(slots, first, group, 0)
        tile_rows = jnp.maximum(places[:, 0], 0)
        tile_cols = jnp.maximum(places[:, 1], 0)
        active = places[:, 0] >= 0
        active = (
            active
            & (tile_cols * tile_size < first_row + row_count)
            & ((tile_cols + 1) * tile_size > first_row)
        )
        picked = stacked[tile_rows]
        products = jnp.einsum("gij,gif->gjf", tiles, picked, preferred_element_type=jnp.float32)
        products = jnp.where(active[:, None, None], products, jnp.float32(0.0))
        return totals.at[tile_cols].add(products)

    start = jnp.zeros((col_tiles, tile_size, width), jnp.float32)
    totals = lax.fori_loop(0, slot_turns(slots, group), turn, start)
    return totals.reshape(out_rows, width)


def shards(features, degrees, proj_weight, bias, grad_out, tile_slots, tile_values):
    slots = tile_slots[0, 0]
    values = tile_values[0, 0]
    row_count = lax.axis_size("row")
    col_count = lax.axis_size("col")
    node_rows = features.shape[0]
    block_rows = col_count * node_rows
    out_rows = row_count * node_rows
    norm = lax.rsqrt(degrees.astype(jnp.float32))
    scaled_in = (features.astype(jnp.float32) * norm[:, None]).astype(jnp.bfloat16)
    cols_in = lax.all_gather(scaled_in, "row", axis=0, tiled=True)
    terms_in = aggregate(cols_in, values, slots, block_rows)
    smooth = lax.psum_scatter(terms_in, "col", scatter_dimension=0, tiled=True)
    smoothed = (norm[:, None] * smooth).astype(jnp.bfloat16)
    pre = jnp.dot(smoothed, proj_weight, preferred_element_type=jnp.float32) + bias[None, :]
    activations, backward = jax.vjp(gelu_tanh, pre)
    dpre = backward(grad_out.astype(jnp.float32))[0]
    dpre_b = dpre.astype(jnp.bfloat16)
    factor = (node_rows * row_count * col_count) ** (-0.5)
    grad_weight = (
        lax.dot_general(
            smoothed, dpre_b, (((0,), (0,)), ((), ())), preferred_element_type=jnp.float32
        )
        * factor
    )
    grad_bias = jnp.sum(dpre, axis=0) * factor
    projected = lax.dot_general(
        dpre_b, proj_weight, (((1,), (1,)), ((), ())), preferred_element_type=jnp.float32
    )
    back_in = (projected * norm[:, None]).astype(jnp.bfloat16)
    rows_in = lax.all_gather(back_in, "col", axis=0, tiled=True)
    back_terms = aggregate_back(rows_in, values, slots, out_rows, 0, out_rows)
    back_sum = lax.psum_scatter(back_terms, "row", scatter_dimension=0, tiled=True)
    grad_features = (norm[:, None] * back_sum).astype(jnp.bfloat16)
    grad_weight, grad_bias = lax.psum((grad_weight, grad_bias), ("row", "col"))
    return (activations.astype(jnp.bfloat16), grad_weight, grad_bias, grad_features)


def solution(mesh):
    return jax.shard_map(
        shards,
        mesh=mesh,
        in_specs=(
            P(("row", "col"), None),
            P(("row", "col")),
            P(),
            P(),
            P(("row", "col"), None),
            P("row", "col", None, None),
            P("row", "col", None, None, None),
        ),
        out_specs=(P(("row", "col"), None), P(), P(), P(("row", "col"), None)),
        check_vma=False,
    )
```

profile of v0, /device:TPU:1, one launch (start us, length us, event | category | flops | bytes accessed | tf_op | source)
XLA Modules:
  0.0 759.0 jit_solution(12490134073901007828)
XLA Ops:
  7.2 0.0 copy-start
  7.2 0.0 all-gather.2.cloned.1.call-start
  7.2 0.7 convert_rsqrt_fusion
  7.9 1.5 multiply_convert_fusion.3
  9.4 0.0 all-gather.2.cloned.1.call-update
  9.4 0.0 reduce-scatter.3.cloned.1.call-start
  9.4 74.0 %all-gather.2.cloned.1.call-done = bf16[4096,128]{1,0:T(8,128)(2,1)} async-done(((bf16[128,128]{1,0:T(8,128)(2,1)}), bf16[4096,128]{1,0:T(8,128)(2,1)}) %all-gather.2.cloned.1.call-update) | async-done | bytes 1048592 | tf_op jit(solution)/shard_map/all_gather | solution.py:80
  83.4 0.1 broadcast_in_dim.77
  83.5 19.4 %while.26 = (s32[]{:T(128)}, f32[16,128,128]{2,1,0:T(8,128)S(1)}, s32[32,2]{0,1:T(2,128)}, bf16[32,128,128]{2,1,0:T(8,128)(2,1)}, bf16[32,128,128]{2,1,0:T(8,128...) while((s32[]{:T(128)}, f32[16,128,128]{2,1,0:T(8,128)S(1)}, s32[32,2]{0,1:T(2,128)}, ...), condition=%wide.region_2.3_spmd, body=%wide.region_0.2_spmd.sunk | while | flops 33817628 | bytes 3150371 | solution.py:37
  83.6 0.8 constant_dynamic-slice_fusion.4
  84.3 1.8 gather_fusion
  86.2 1.2 convolution_select_fusion.4
  87.4 1.0 scatter_fusion
  88.4 0.8 constant_dynamic-slice_fusion.4
  89.2 1.8 gather_fusion
  91.0 1.2 convolution_select_fusion.4
  92.2 1.0 scatter_fusion
  93.3 0.8 constant_dynamic-slice_fusion.4
  94.1 1.8 gather_fusion
  95.9 1.2 convolution_select_fusion.4
  97.1 1.0 scatter_fusion
  98.1 0.8 constant_dynamic-slice_fusion.4
  98.9 1.8 gather_fusion
  100.7 1.2 convolution_select_fusion.4
  101.9 1.0 scatter_fusion
  103.0 0.0 copy-start.8
  103.0 0.0 copy-start.9
  103.0 1.0 copy-done.2
  104.0 0.0 reduce-scatter.3.cloned.1.call-update
  104.0 0.0 reduce-scatter.5.cloned.1.call-start
  104.1 2.3 copy.11
  106.3 195.9 %reduce-scatter.3.cloned.1.call-done = f32[128,128]{1,0:T(8,128)} async-done(((f32[2048,128]{1,0:T(8,128)}), f32[128,128]{1,0:T(8,128)}) %reduce-scatter.3.cloned.1.call-update) | async-done | bytes 65552 | tf_op jit(solution)/shard_map/reduce_scatter | solution.py:82
  302.3 2.5 fusion.17
  304.8 0.2 fusion.5
  305.0 34.1 %all_gather.7 = bf16[2048,128]{1,0:T(8,128)(2,1)S(1)} all-gather(bf16[128,128]{1,0:T(8,128)(2,1)S(1)} %fusion.5), channel_id=1, replica_groups=mesh['row'=32,'col'=16] {'col'}, dimensions={0}, use_global_device_ids=true | all-gather | bytes 557056 | tf_op jit(solution)/shard_map/all_gather | solution.py:100
  339.0 0.2 broadcast_in_dim.78
  339.3 11.9 %while.27 = (s32[]{:T(128)}, f32[32,128,128]{2,1,0:T(8,128)S(1)}, s32[32,2]{0,1:T(2,128)S(1)}, bf16[32,128,128]{1,2,0:T(8,128)(2,1)}, bf16[16,128,128]{2,1,0:T(8...) while((s32[]{:T(128)}, f32[32,128,128]{2,1,0:T(8,128)S(1)}, s32[32,2]{0,1:T(2,128)S(1)}, ...), condition=%wide.region_9.10_spmd, body=%wide.region_7.0_spmd.sunk | while | flops 33817692 | bytes 3150403 | solution.py:66
  339.3 0.1 constant_dynamic-slice_fusion.5
  339.4 0.6 gather_fusion.1
  340.0 1.2 convolution_select_fusion.5
  341.2 1.0 scatter_fusion.1
  342.3 0.1 constant_dynamic-slice_fusion.5
  342.4 0.6 gather_fusion.1
  343.0 1.2 convolution_select_fusion.5
  344.2 1.0 scatter_fusion.1
  345.2 0.1 constant_dynamic-slice_fusion.5
  345.4 0.6 gather_fusion.1
  346.0 1.2 convolution_select_fusion.5
  347.2 1.0 scatter_fusion.1
  348.2 0.1 constant_dynamic-slice_fusion.5
  348.3 0.6 gather_fusion.1
  348.9 1.2 convolution_select_fusion.5
  350.1 1.0 scatter_fusion.1
  351.2 0.0 copy-start.7
  351.2 1.3 copy-done.1
  352.5 0.0 reduce-scatter.5.cloned.1.call-update
  352.5 0.0 all-reduce.2.cloned.1.call-start
  352.6 108.8 %psum.15 = f32[512]{0:T(512)} all-reduce(f32[512]{0:T(512)S(1)} %broadcast_multiply_fusion), channel_id=1, replica_groups=mesh['row'=32,'col'=16] {'row','col'}, use_global_device_ids=true, to_apply=%region_6.0 | all-reduce | flops 512 | bytes 4096 | tf_op jit(solution)/shard_map/psum | solution.py:104
  461.5 1.0 convolution_multiply_fusion
  462.4 0.0 all-reduce.2.cloned.1.call-update
  462.5 15.8 %reduce-scatter.5.cloned.1.call-done = f32[128,128]{1,0:T(8,128)} async-done(((f32[4096,128]{1,0:T(8,128)}), f32[128,128]{1,0:T(8,128)}) %reduce-scatter.5.cloned.1.call-update) | async-done | bytes 65552 | tf_op jit(solution)/shard_map/reduce_scatter | solution.py:102
  478.3 1.5 multiply_convert_fusion.1
  479.8 271.0 %all-reduce.2.cloned.1.call-done = f32[128,512]{1,0:T(8,128)} async-done(((f32[128,512]{1,0:T(8,128)}), f32[128,512]{1,0:T(8,128)}) %all-reduce.2.cloned.1.call-update) | async-done | bytes 262160 | tf_op jit(solution)/shard_map/psum | solution.py:104
  750.8 1.7 copy.29
  (39 shorter events, 0.2 us)
Async XLA Ops:
  7.2 295.1 %copy-start = (bf16[128,512]{1,0:T(8,128)(2,1)S(1)}, bf16[128,512]{1,0:T(8,128)(2,1)}, u32[]{:S(2)}) copy-start(bf16[128,512]{1,0:T(8,128)(2,1)} %param.13) | copy-start | bytes 393220
  7.2 76.3 %all-gather.2.cloned.1.call-start = ((), (), s32[]{:S(2)}) async-start(), calls=%async_computation.2 | async-start | bytes 1081344 | tf_op jit(solution)/shard_map/all_gather | solution.py:80
  9.4 292.9 %reduce-scatter.3.cloned.1.call-start = ((), (), s32[]{:S(2)}) async-start(), calls=%async_computation.3 | async-start | bytes 1114112 | tf_op jit(solution)/shard_map/reduce_scatter | solution.py:82
  102.9 1.0 copy-start.2
  103.0 199.3 %copy-start.8 = (bf16[128,512]{1,0:T(8,128)(2,1)S(1)}, bf16[128,512]{1,0:T(8,128)(2,1)}, u32[]{:S(2)}) copy-start(bf16[128,512]{1,0:T(8,128)(2,1)} %param.15) | copy-start | bytes 393220
  103.0 199.3 %copy-start.9 = (f32[512]{0:T(512)S(1)}, f32[512]{0:T(512)}, u32[]{:S(2)}) copy-start(f32[512]{0:T(512)} %param.14) | copy-start | bytes 6148
  104.0 374.3 %reduce-scatter.5.cloned.1.call-start = ((), (), s32[]{:S(2)}) async-start(), calls=%async_computation.5 | async-start | bytes 2162688 | tf_op jit(solution)/shard_map/reduce_scatter | solution.py:102
  106.3 232.9 %copy-start.5 = (s32[32,2]{0,1:T(2,128)S(1)}, s32[32,2]{0,1:T(2,128)}, u32[]{:S(2)}) copy-start(s32[32,2]{0,1:T(2,128)} %get-tuple-element.372) | copy-start | bytes 772
  304.8 34.3 %copy-start.3 = (bf16[128,512]{1,0:T(8,128)(2,1)}, bf16[128,512]{1,0:T(8,128)(2,1)S(1)}, u32[]{:S(2)}) copy-start(bf16[128,512]{1,0:T(8,128)(2,1)S(1)} %get-tuple-element.220) | copy-start | bytes 393220
  351.2 1.4 copy-start.1
  351.2 1.4 copy-start.7
  351.2 110.3 %copy-start.4 = (bf16[128,512]{1,0:T(8,128)(2,1)S(1)}, bf16[128,512]{1,0:T(8,128)(2,1)}, u32[]{:S(2)}) copy-start(bf16[128,512]{1,0:T(8,128)(2,1)} %copy-done.3) | copy-start | bytes 393220
  351.2 110.3 %copy-start.6 = (f32[128,128]{1,0:T(8,128)S(1)}, f32[128,128]{1,0:T(8,128)}, u32[]{:S(2)}) copy-start(f32[128,128]{1,0:T(8,128)} %reduce-scatter.3.cloned.1.call-done) | copy-start | bytes 196612
  352.5 398.3 %all-reduce.2.cloned.1.call-start = ((), (), s32[]{:S(2)}) async-start(), calls=%async_computation.4 | async-start | bytes 524288 | tf_op jit(solution)/shard_map/psum | solution.py:104
Sparse Core Ops, SparseCore 0:
  10.7 72.6 all-gather.1
  104.1 198.0 reduce-scatter.2
  352.7 125.5 reduce-scatter.4
  484.5 266.3 all-reduce.1
where the time goes:
time: 760 us; the launch traced here: 759 us
  waiting for transfers between devices  557 us (73%)
  blocking collectives  143 us (19%)
  local copies, waits for them, and re-layouts  19.6 us (3%)
  between operations  13.9 us (2%)
  matrix products  13.1 us (2%)
  other arithmetic  12.1 us (2%)
    psum x1, waiting for transfers between devices, shards(): grad_weight, grad_bias = lax.psum((grad_weight, grad_bias), ('row', 'col'))  271 us
    reduce_scatter x1, waiting for transfers between devices, shards(): smooth = lax.psum_scatter(terms_in, 'col', scatter_dimension=0, tiled=True)  196 us
    psum x1, blocking collectives, shards(): grad_weight, grad_bias = lax.psum((grad_weight, grad_bias), ('row', 'col'))  109 us
    all_gather x1, waiting for transfers between devices, shards(): cols_in = lax.all_gather(scaled_in, 'row', axis=0, tiled=True)  74 us
    all_gather x1, blocking collectives, shards(): rows_in = lax.all_gather(back_in, 'col', axis=0, tiled=True)  34.1 us
    reduce_scatter x1, waiting for transfers between devices, shards(): lax.psum_scatter(back_terms, 'row', scatter_dimension=0, tiled=True)  15.8 us
  transfers between devices with their start and end apart: 4, of which 4 were waited for; matrix products, arithmetic and copies ran while one was open for 1% of the time, Pallas kernels for 0%

commit v1 on v0

v1 whole, which is shorter than its diff:
```python
import jax
import jax.numpy as jnp
from jax import lax
from jax.experimental import pallas as pl
from jax.experimental.pallas import tpu as pltpu
from jax.sharding import PartitionSpec as P

MESH = pl.DeviceIdType.MESH
BF16 = jnp.bfloat16
F32 = jnp.float32

N = 128
HID = 512
K = 32
NZ = 8
FAR = (4, 3, 5, 2, 6, 1, 7)
NEAR = (1, 7, 2, 6, 3, 5, 4)
PERM, COLP, KEEPF, LASTR, HASR = 0, 32, 64, 96, 112
ROWK, KEEPB, LASTC, HASC = 128, 160, 192, 224


def index_table(slots):
    rows, cols = slots[:, 0], slots[:, 1]
    live = rows >= 0
    k = jnp.arange(K, dtype=jnp.int32)
    row_key = jnp.where(live, rows, 16)
    key = row_key * K + k
    rank = jnp.sum((key[None, :] < key[:, None]).astype(jnp.int32), axis=1)
    chosen = rank[None, :] == k[:, None]

    def pick(values):
        return jnp.sum(jnp.where(chosen, values[None, :], 0), axis=1)

    perm, colp, rowp = pick(k), pick(jnp.maximum(cols, 0)), pick(row_key)
    keepf = jnp.concatenate([jnp.zeros((1,), jnp.int32), (rowp[1:] == rowp[:-1]).astype(jnp.int32)])
    col_key = jnp.where(live, cols, 32)
    keepb = jnp.concatenate([jnp.zeros((1,), jnp.int32), (col_key[1:] == col_key[:-1]).astype(jnp.int32)])

    def ends(keys, count):
        places = jnp.arange(count, dtype=jnp.int32)[:, None]
        last = jnp.sum((keys[None, :] <= places).astype(jnp.int32), axis=1) - 1
        has = jnp.max((keys[None, :] == places).astype(jnp.int32), axis=1)
        return jnp.maximum(last, 0), has

    lastr, hasr = ends(row_key, 16)
    lastc, hasc = ends(col_key, 32)
    return jnp.concatenate([perm, colp, keepf, lastr, hasr, jnp.maximum(rows, 0), keepb, lastc, hasc])


def layer(tab, feat, deg, w, bias, gout, vals_hbm,
          act, gw, gb, gf,
          vals, xg, ps, xs2, xr2, ys2, yr2, own2, dpre, bt,
          ss5, sr5, xs5, xr5, zs5, zr5, own5,
          gwx, arh_in, arh, zb, yb, xb, gwo,
          load_sem, s1z, r1z, s1x, r1x, s1s, r1s, s2x, r2x, s2y, r2y,
          s4y, r4y, s4x, r4x, s5s, r5s, s5x, r5x, s5z, r5z,
          sa, ra, sbz, rbz, scy, rcy, sdx, rdx, sez, rez, sf, rf):
    row, col = lax.axis_index("row"), lax.axis_index("col")
    x, z, k = row // 16, (row // 2) % NZ, row % 2
    h, y = col // NZ, col % NZ

    def leaf(x_, z_, k_):
        return (x_ * NZ + z_) * 2 + k_

    def zdev(d):
        return (leaf(x, (z + d) % NZ, k), col)

    def ydev(d):
        return (row, h * NZ + (y + d) % NZ)

    sib = (leaf(x, z, 1 - k), col)
    xl = (leaf(1 - x, z, k), col)
    xh = (row, (1 - h) * NZ + y)
    xlh = (leaf(1 - x, z, k), (1 - h) * NZ + y)

    def copy(src, dst, ssem, rsem, dev):
        return pltpu.make_async_remote_copy(
            src_ref=src, dst_ref=dst, send_sem=ssem, recv_sem=rsem, device_id=dev, device_id_type=MESH)

    sent = []

    def send(src, dst, ssem, rsem, dev):
        cp = copy(src, dst, ssem, rsem, dev)
        cp.start()
        sent.append(cp)

    def arrive(dst, ssem, rsem):
        copy(dst, dst, ssem, rsem, sib).wait_recv()

    barrier = pltpu.get_barrier_semaphore()
    partners = [sib, xl, xh, xlh] + [zdev(d) for d in NEAR] + [ydev(d) for d in NEAR]
    for dev in partners:
        pl.semaphore_signal(barrier, inc=1, device_id=dev, device_id_type=MESH)
    load = pltpu.make_async_copy(vals_hbm, vals, load_sem)
    load.start()

    nrow = lax.rsqrt(deg[...].astype(F32))
    ncol = jnp.broadcast_to(nrow, (N, N)).T
    xg[row] = (feat[...].astype(F32) * ncol).astype(BF16)
    pl.semaphore_wait(barrier, len(partners))

    for d in FAR:
        send(xg.at[row], xg.at[row], s1z.at[d], r1z.at[d], zdev(d))
    send(xg.at[row], xg.at[row], s1x.at[0], r1x.at[0], xl)
    send(xg.at[row], xg.at[row], s1s.at[0], r1s.at[0], sib)

    def from_z(d):
        at = leaf(x, (z + NZ - d) % NZ, k)
        arrive(xg.at[at], s1z.at[d], r1z.at[d])
        send(xg.at[at], xg.at[at], s1x.at[d], r1x.at[d], xl)
        send(xg.at[at], xg.at[at], s1s.at[d], r1s.at[d], sib)

    def from_x(d):
        at = leaf(1 - x, (z + NZ - d) % NZ, k)
        arrive(xg.at[at], s1x.at[d], r1x.at[d])
        send(xg.at[at], xg.at[at], s1s.at[NZ + d], r1s.at[NZ + d], sib)

    from_z(1), from_z(7), from_x(0), from_z(2), from_z(6), from_x(1), from_x(7)
    from_z(3), from_z(5), from_x(2), from_x(6), from_z(4), from_x(3), from_x(5), from_x(4)
    for d in (0,) + NEAR:
        arrive(xg.at[leaf(x, (z + NZ - d) % NZ, 1 - k)], s1s.at[d], r1s.at[d])
    for d in (0,) + NEAR:
        arrive(xg.at[leaf(1 - x, (z + NZ - d) % NZ, 1 - k)], s1s.at[NZ + d], r1s.at[NZ + d])
    load.wait()

    def forward_turn(turn, total):
        for i in range(8):
            p = turn * 8 + i
            product = jnp.dot(vals[tab[0, PERM + p]], xg[tab[0, COLP + p]], preferred_element_type=F32)
            total = total * tab[0, KEEPF + p].astype(F32) + product
            ps[p] = total
        return total

    lax.fori_loop(0, K // 8, forward_turn, jnp.zeros((N, N), F32))

    def row_sum(at):
        return ps[tab[0, LASTR + at]] * tab[0, HASR + at].astype(F32)

    for d in FAR + (0,):
        xs2[d] = row_sum((1 - h) * NZ + (y + d) % NZ).astype(BF16)
        send(xs2.at[d], xr2.at[d], s2x.at[d], r2x.at[d], xh)
    for d in FAR + (0,):
        mine = row_sum(h * NZ + (y + d) % NZ)
        arrive(xr2.at[d], s2x.at[d], r2x.at[d])
        both = mine + xr2[d].astype(F32)
        if d:
            ys2[d] = both.astype(BF16)
            send(ys2.at[d], yr2.at[d], s2y.at[d], r2y.at[d], ydev(d))
        else:
            own2[...] = both
    smooth = own2[...]
    for d in NEAR:
        arrive(yr2.at[d], s2y.at[d], r2y.at[d])
        smooth = smooth + yr2[d].astype(F32)

    scaled = smooth * ncol
    smoothed = scaled.astype(BF16)
    gwx[...] = jnp.zeros((N, HID + N), F32)
    for c in range(HID // N):
        cs = slice(c * N, (c + 1) * N)
        pre = jnp.dot(smoothed, w[:, cs], preferred_element_type=F32) + bias[:, cs]
        square = pre * pre
        slope = 0.7978845608028654
        t = jnp.tanh(slope * (pre + 0.044715 * (square * pre)))
        half = 0.5 * (1.0 + t)
        act[:, cs] = (pre * half).astype(BF16)
        slant = half + (0.5 * slope) * pre * (1.0 - t * t) * (1.0 + (3 * 0.044715) * square)
        dp = gout[:, cs].astype(F32) * slant
        gwx[c:c + 1, HID:] = jnp.sum(dp, axis=0, keepdims=True)
        dpre[:, cs] = dp.astype(BF16)
    projected = lax.dot_general(w[...], dpre[...], (((1,), (1,)), ((), ())), preferred_element_type=F32)
    bt[col] = (projected * nrow).astype(BF16)

    for d in FAR:
        send(bt.at[col], bt.at[col], s4y.at[d], r4y.at[d], ydev(d))
    send(bt.at[col], bt.at[col], s4x.at[0], r4x.at[0], xh)
    gwx[:, :HID] = jnp.dot(scaled.T.astype(BF16), dpre[...], preferred_element_type=F32)
    send(gwx.at[pl.ds((1 - k) * 64, 64)], arh_in, sa, ra, sib)
    for d in NEAR:
        at = h * NZ + (y + NZ - d) % NZ
        arrive(bt.at[at], s4y.at[d], r4y.at[d])
        send(bt.at[at], bt.at[at], s4x.at[d], r4x.at[d], xh)
    arrive(arh_in, sa, ra)
    arh[...] = gwx[pl.ds(pl.multiple_of(k * 64, 64), 64)] + arh_in[...]
    for d in FAR:
        at = pl.multiple_of(((z + d) % NZ) * 8, 8)
        send(arh.at[pl.ds(at, 8)], zb.at[d], sbz.at[d], rbz.at[d], zdev(d))
    for d in (0,) + NEAR:
        arrive(bt.at[(1 - h) * NZ + (y + NZ - d) % NZ], s4x.at[d], r4x.at[d])

    def back_turn(turn, total):
        for i in range(8):
            p = turn * 8 + i
            product = jnp.dot(bt[tab[0, ROWK + p]], vals[p], preferred_element_type=F32)
            total = total * tab[0, KEEPB + p].astype(F32) + product
            ps[p] = total
        return total

    lax.fori_loop(0, K // 8, back_turn, jnp.zeros((N, N), F32))

    def col_sum(at):
        return ps[tab[0, LASTC + at]] * tab[0, HASC + at].astype(F32)

    for a in (1, 0):
        xa = 1 - x if a else x
        for d in range(NZ):
            ss5[a, d] = col_sum(leaf(xa, (z + d) % NZ, 1 - k)).astype(BF16)
        send(ss5.at[a], sr5.at[a], s5s.at[a], r5s.at[a], sib)
    chunk = arh[pl.ds(pl.multiple_of(z * 8, 8), 8)]
    for d in NEAR:
        arrive(zb.at[d], sbz.at[d], rbz.at[d])
        chunk = chunk + zb[d]
    yb[y] = chunk
    for d in FAR:
        send(yb.at[y], yb.at[y], scy.at[d], rcy.at[d], ydev(d))
    arrive(sr5.at[1], s5s.at[1], r5s.at[1])
    for d in FAR + (0,):
        xs5[d] = (col_sum(leaf(1 - x, (z + d) % NZ, k)) + sr5[1, d].astype(F32)).astype(BF16)
        send(xs5.at[d], xr5.at[d], s5x.at[d], r5x.at[d], xl)
    arrive(sr5.at[0], s5s.at[0], r5s.at[0])
    for d in FAR + (0,):
        mine = col_sum(leaf(x, (z + d) % NZ, k)) + sr5[0, d].astype(F32)
        arrive(xr5.at[d], s5x.at[d], r5x.at[d])
        both = mine + xr5[d].astype(F32)
        if d:
            zs5[d] = both.astype(BF16)
            send(zs5.at[d], zr5.at[d], s5z.at[d], r5z.at[d], zdev(d))
        else:
            own5[...] = both
    for d in NEAR:
        arrive(yb.at[(y + NZ - d) % NZ], scy.at[d], rcy.at[d])
    chunk = yb[0]
    for i in range(1, NZ):
        chunk = chunk + yb[i]
    me = x * 2 + h
    xb[me] = chunk
    send(xb.at[me], xb.at[me], sdx.at[0], rdx.at[0], xl)
    send(xb.at[me], xb.at[me], sdx.at[1], rdx.at[1], xh)
    send(xb.at[me], xb.at[me], sdx.at[2], rdx.at[2], xlh)
    arrive(xb.at[(1 - x) * 2 + h], sdx.at[0], rdx.at[0])
    arrive(xb.at[x * 2 + 1 - h], sdx.at[1], rdx.at[1])
    arrive(xb.at[(1 - x) * 2 + 1 - h], sdx.at[2], rdx.at[2])
    mine = pl.ds(pl.multiple_of((k * NZ + z) * 8, 8), 8)
    gwo[mine] = ((xb[0] + xb[1]) + (xb[2] + xb[3])) * (65536.0 ** -0.5)
    for d in FAR:
        send(gwo.at[mine], gwo.at[mine], sez.at[d], rez.at[d], zdev(d))
    back = own5[...]
    for d in NEAR:
        arrive(zr5.at[d], s5z.at[d], r5z.at[d])
        back = back + zr5[d].astype(F32)
    gf[...] = (back * nrow).T.astype(BF16)
    for d in NEAR:
        at = pl.ds(pl.multiple_of((k * NZ + (z + NZ - d) % NZ) * 8, 8), 8)
        arrive(gwo.at[at], sez.at[d], rez.at[d])
    ours, theirs = pl.ds(pl.multiple_of(k * 64, 64), 64), pl.ds(pl.multiple_of((1 - k) * 64, 64), 64)
    send(gwo.at[ours], gwo.at[ours], sf, rf, sib)
    arrive(gwo.at[theirs], sf, rf)
    gw[...] = gwo[:, :HID]
    for c in range(HID // N):
        gb[:, c * N:(c + 1) * N] = gwo[c:c + 1, HID:]
    for cp in sent:
        cp.wait_send()


def shards(features, degrees, proj_weight, bias, grad_out, tile_slots, tile_values):
    table = index_table(tile_slots[0, 0]).reshape(1, 256)
    vmem = pl.BlockSpec(memory_space=pltpu.VMEM)
    sem = pltpu.SemaphoreType.DMA
    tile = lambda *lead: pltpu.VMEM(lead + (N, N), BF16)
    wide = lambda *lead: pltpu.VMEM(lead + (HID + N,), F32)
    act, gw, gb, gf = pl.pallas_call(
        layer,
        name="layer",
        out_shape=(
            jax.ShapeDtypeStruct((N, HID), BF16),
            jax.ShapeDtypeStruct((N, HID), F32),
            jax.ShapeDtypeStruct((1, HID), F32),
            jax.ShapeDtypeStruct((N, N), BF16),
        ),
        in_specs=[pl.BlockSpec(memory_space=pltpu.SMEM)] + [vmem] * 5 + [pl.BlockSpec(memory_space=pl.ANY)],
        out_specs=(vmem,) * 4,
        scratch_shapes=[
            tile(K), tile(32), pltpu.VMEM((K, N, N), F32),
            tile(8), tile(8), tile(8), tile(8), pltpu.VMEM((N, N), F32),
            pltpu.VMEM((N, HID), BF16), tile(16),
            tile(2, 8), tile(2, 8), tile(8), tile(8), tile(8), tile(8), pltpu.VMEM((N, N), F32),
            wide(N), wide(64), wide(64), wide(8, 8), wide(8, 8), wide(4, 8), wide(N),
            sem, sem((8,)), sem((8,)), sem((8,)), sem((8,)), sem((16,)), sem((16,)),
            sem((8,)), sem((8,)), sem((8,)), sem((8,)),
            sem((8,)), sem((8,)), sem((8,)), sem((8,)),
            sem((2,)), sem((2,)), sem((8,)), sem((8,)), sem((8,)), sem((8,)),
            sem, sem, sem((8,)), sem((8,)), sem((8,)), sem((8,)), sem((3,)), sem((3,)),
            sem((8,)), sem((8,)), sem, sem,
        ],
        compiler_params=pltpu.CompilerParams(
            collective_id=0, has_side_effects=True, vmem_limit_bytes=40 << 20),
        cost_estimate=pl.CostEstimate(flops=3 * 10 ** 8, bytes_accessed=2 * 10 ** 6, transcendentals=65536),
    )(table, features, degrees.reshape(1, N), proj_weight, bias.reshape(1, HID), grad_out, tile_values[0, 0])
    return act, gw, gb.reshape(HID), gf


def solution(mesh):
    leaf = P(("row", "col"))
    leaf_rows = P(("row", "col"), None)
    return jax.shard_map(
        shards,
        mesh=mesh,
        in_specs=(leaf_rows, leaf, P(), P(), leaf_rows, P("row", "col", None, None), P("row", "col", None, None, None)),
        out_specs=(leaf_rows, P(), P(), leaf_rows),
        check_vma=False,
    )
```

time: 760 us -> 92.4 us (0.12)
  waiting for transfers between devices: 557 us -> 0 us
  blocking collectives: 143 us -> 0 us
  Pallas kernels: 0 us -> 83 us
  local copies, waits for them, and re-layouts: 19.6 us -> 6.32 us
  between operations: 13.9 us -> 0.69 us
  matrix products: 13.1 us -> 0 us
  other arithmetic: 12.1 us -> 2.09 us
    psum x1 -> x0, waiting for transfers between devices: 271 us -> none  [shards(): grad_weight, grad_bias = lax.psum((grad_weight, grad_bias), ('row', 'col'))]
    reduce_scatter x2 -> x0, waiting for transfers between devices: 212 us -> none  [the longest x1 196 us: shards(): smooth = lax.psum_scatter(terms_in, 'col', scatter_dimension=0, tiled=True)]
    psum x1 -> x0, blocking collectives: 109 us -> none  [shards(): grad_weight, grad_bias = lax.psum((grad_weight, grad_bias), ('row', 'col'))]
    pallas_call x0 -> x1, Pallas kernels: none -> 83 us  [shards(): pl.pallas_call(layer, name='layer', out_shape=(jax.ShapeDtypeStruct((N, H...]
    all_gather x1 -> x0, waiting for transfers between devices: 74 us -> none  [shards(): cols_in = lax.all_gather(scaled_in, 'row', axis=0, tiled=True)]
    all_gather x1 -> x0, blocking collectives: 34.1 us -> none  [shards(): rows_in = lax.all_gather(back_in, 'col', axis=0, tiled=True)]
    dot_general x11 -> x0, matrix products: 13.1 us -> none  [the longest x4 4.73 us: turn(): jnp.einsum('gij,gif->gjf', tiles, picked, preferred_element_type=jnp.floa...]
    gather x8 -> x0, local copies, waits for them, and re-layouts: 9.68 us -> none  [the longest x4 7.29 us: turn(): picked = stacked[tile_cols]]
  transfers between devices with their start and end apart: 4 -> 0, of which waited for: 4 -> 0; matrix products, arithmetic and copies ran while one was open for 1% -> 0% of each run, Pallas kernels for 0% -> 0%
where the time goes in v1:
time: 92.4 us; the launch traced here: 92.1 us
  Pallas kernels  83 us (90%)
  local copies, waits for them, and re-layouts  6.32 us (7%)
  other arithmetic  2.09 us (2%)
    pallas_call x1, Pallas kernels, shards(): pl.pallas_call(layer, name='layer', out_shape=(jax.ShapeDtypeStruct((N, H...  83 us
    unnamed x16, local copies, waits for them, and re-layouts  6.24 us

profile of v1, /device:TPU:1, one launch (start us, length us, event | category | flops | bytes accessed | tf_op | source)
XLA Modules:
  0.0 92.1 jit_solution(11273610036741934525)
XLA Ops:
  0.6 0.0 copy-start.3
  0.6 0.7 fusion.2
  1.3 0.8 compare_select_fusion.1
  2.1 0.2 convert_reduce_fusion.2
  2.3 0.1 compare_convert_fusion
  2.3 0.2 convert_reduce_fusion
  2.5 0.1 compare_convert_fusion.1
  2.6 0.1 convert_reduce_fusion.3
  2.7 0.0 copy-start.4
  2.8 0.1 concatenate.3
  2.8 0.0 copy-start.5
  2.8 0.0 copy-done.3
  2.9 0.6 copy-done.4
  3.4 0.1 copy-done.5
  3.5 0.0 copy-start
  3.5 1.2 %copy-done = bf16[1,1,32,128,128]{4,3,2,1,0:T(8,128)(2,1)S(1)} copy-done((bf16[1,1,32,128,128]{4,3,2,1,0:T(8,128)(2,1)S(1)}, bf16[1,1,32,128,128]{4,3,2,1,0:T(8,128)(2,1)}, u32[]{:S(2)}) %copy-start) | copy-done | bytes 1048600
  4.7 0.0 copy-start.1
  4.7 0.9 copy-done.1
  5.6 0.0 copy-start.2
  5.6 0.9 copy-done.2
  6.5 83.0 %layer.1 = (bf16[128,512]{1,0:T(8,128)(2,1)S(1)}, f32[128,512]{1,0:T(8,128)S(1)}, f32[1,512]{1,0:T(1,128)S(1)}, bf16[128,128]{1,0:T(8,128)(2,1)S(1)}) custom-call(s32[1,256]{1,0:T(1,128)S(1)} %bitcast.18, bf16[128,128]{1,0:T(8,128)(2,1)S(1)} %copy-done.3, s32[1,128]{1,0:T(1,128)S(1)} %bitcast.21, bf16[128,512]{1,0:T(8,128)(2,1)S(1)} %copy-done.1, ...), custom_call_target="tpu_custom_call" | custom-call | flops 300000000 | bytes 2000000 | tf_op jit(solution)/shard_map/layer/pallas_call | solution.py:271
  89.6 0.7 copy.15
  90.2 0.7 copy.16
  90.9 0.6 copy.17
  91.5 0.6 copy.18
  (2 shorter events, 0.0 us)
Async XLA Ops:
  0.6 2.2 %copy-start.3 = (bf16[128,128]{1,0:T(8,128)(2,1)S(1)}, bf16[128,128]{1,0:T(8,128)(2,1)}, u32[]{:S(2)}) copy-start(bf16[128,128]{1,0:T(8,128)(2,1)} %feat.1) | copy-start | bytes 98308
  2.7 0.7 copy-start.4
  2.8 0.7 copy-start.5
  3.5 1.2 %copy-start = (bf16[1,1,32,128,128]{4,3,2,1,0:T(8,128)(2,1)S(1)}, bf16[1,1,32,128,128]{4,3,2,1,0:T(8,128)(2,1)}, u32[]{:S(2)}) copy-start(bf16[1,1,32,128,128]{4,3,2,1,0:T(8,128)(2,1)} %param.13) | copy-start | bytes 3145732
  4.7 0.9 copy-start.1
  5.6 0.9 copy-start.2

commit v2 on v1

--- a/solution.py
+++ b/solution.py
@@ -6,6 +6,7 @@
 from jax.sharding import PartitionSpec as P
 
 MESH = pl.DeviceIdType.MESH
+VMEM_LIMIT = 57 * 10 ** 6
 BF16 = jnp.bfloat16
 F32 = jnp.float32
 
@@ -15,41 +16,49 @@
 NZ = 8
 FAR = (4, 3, 5, 2, 6, 1, 7)
 NEAR = (1, 7, 2, 6, 3, 5, 4)
-PERM, COLP, KEEPF, LASTR, HASR = 0, 32, 64, 96, 112
-ROWK, KEEPB, LASTC, HASC = 128, 160, 192, 224
+MIXED = (2, 6, 1, 7, 4, 3, 5)
+PERM, COLP, KEEPF, LASTR, HASR, ROWK, KEEPB, LASTC, HASC = range(9)
 
 
 def index_table(slots):
-    rows, cols = slots[:, 0], slots[:, 1]
+    rows, cols = slots[0:1, :], slots[1:2, :]
+    down = lax.broadcasted_iota(jnp.int32, (K, K), 0)
+    along = lax.broadcasted_iota(jnp.int32, (K, K), 1)
     live = rows >= 0
-    k = jnp.arange(K, dtype=jnp.int32)
     row_key = jnp.where(live, rows, 16)
-    key = row_key * K + k
-    rank = jnp.sum((key[None, :] < key[:, None]).astype(jnp.int32), axis=1)
-    chosen = rank[None, :] == k[:, None]
-
-    def pick(values):
-        return jnp.sum(jnp.where(chosen, values[None, :], 0), axis=1)
-
-    perm, colp, rowp = pick(k), pick(jnp.maximum(cols, 0)), pick(row_key)
-    keepf = jnp.concatenate([jnp.zeros((1,), jnp.int32), (rowp[1:] == rowp[:-1]).astype(jnp.int32)])
     col_key = jnp.where(live, cols, 32)
-    keepb = jnp.concatenate([jnp.zeros((1,), jnp.int32), (col_key[1:] == col_key[:-1]).astype(jnp.int32)])
-
-    def ends(keys, count):
-        places = jnp.arange(count, dtype=jnp.int32)[:, None]
-        last = jnp.sum((keys[None, :] <= places).astype(jnp.int32), axis=1) - 1
-        has = jnp.max((keys[None, :] == places).astype(jnp.int32), axis=1)
-        return jnp.maximum(last, 0), has
-
-    lastr, hasr = ends(row_key, 16)
-    lastc, hasc = ends(col_key, 32)
-    return jnp.concatenate([perm, colp, keepf, lastr, hasr, jnp.maximum(rows, 0), keepb, lastc, hasc])
-
-
-def layer(tab, feat, deg, w, bias, gout, vals_hbm,
-          act, gw, gb, gf,
-          vals, xg, ps, xs2, xr2, ys2, yr2, own2, dpre, bt,
+
+    def upright(values):
+        return jnp.sum(jnp.where(down == along, jnp.broadcast_to(values, (K, K)), 0), axis=1, keepdims=True)
+
+    def place(values, where):
+        return jnp.sum(jnp.where(where, jnp.broadcast_to(values, (K, K)), 0), axis=0, keepdims=True)
+
+    def count(where):
+        return jnp.sum(where.astype(jnp.int32), axis=0, keepdims=True)
+
+    rows_up, cols_up = upright(row_key), upright(col_key)
+    key_up = rows_up * K + down[:, 0:1]
+    key = row_key * K + along[0:1, :]
+    rank = jnp.sum((jnp.broadcast_to(key, (K, K)) < key_up).astype(jnp.int32), axis=1, keepdims=True)
+    here, after = rank == along, rank + 1 == along
+    row_here = place(rows_up, here)
+    return (
+        place(down[:, 0:1], here),
+        jnp.minimum(place(cols_up, here), 31),
+        (row_here == place(rows_up, after)).astype(jnp.int32),
+        jnp.maximum(count(rows_up <= along) - 1, 0),
+        (count(rows_up == along) > 0).astype(jnp.int32),
+        jnp.minimum(row_key, 15),
+        (col_key == place(cols_up, down + 1 == along)).astype(jnp.int32),
+        jnp.maximum(count(cols_up <= along) - 1, 0),
+        (count(cols_up == along) > 0).astype(jnp.int32),
+    )
+
+
+def layer(slots_hbm, feat_hbm, deg_hbm, w_hbm, bias_hbm, gout_hbm, vals_hbm,
+          act_hbm, gw_hbm, gb_hbm, gf_hbm,
+          act, gw, gb, gf, slots, tabv, tab, feat, deg, w, bias, gout, vals, xg, ps, xs2, xr2, ys2, yr2, own2, dpre, bt,
           ss5, sr5, xs5, xr5, zs5, zr5, own5,
           gwx, arh_in, arh, zb, yb, xb, gwo,
           load_sem, s1z, r1z, s1x, r1x, s1s, r1s, s2x, r2x, s2y, r2y,
@@ -91,18 +100,30 @@
     partners = [sib, xl, xh, xlh] + [zdev(d) for d in NEAR] + [ydev(d) for d in NEAR]
     for dev in partners:
         pl.semaphore_signal(barrier, inc=1, device_id=dev, device_id_type=MESH)
-    load = pltpu.make_async_copy(vals_hbm, vals, load_sem)
-    load.start()
+    loads = []
+    for i, (far, here) in enumerate((
+            (deg_hbm, deg), (feat_hbm, feat), (slots_hbm, slots), (vals_hbm, vals), (w_hbm, w), (bias_hbm, bias),
+            (gout_hbm, gout))):
+        loads.append(pltpu.make_async_copy(far, here, load_sem.at[i]))
+        loads[i].start()
+    loads[0].wait()
+    loads[1].wait()
 
     nrow = lax.rsqrt(deg[...].astype(F32))
     ncol = jnp.broadcast_to(nrow, (N, N)).T
     xg[row] = (feat[...].astype(F32) * ncol).astype(BF16)
     pl.semaphore_wait(barrier, len(partners))
 
-    for d in FAR:
+    for d in MIXED:
         send(xg.at[row], xg.at[row], s1z.at[d], r1z.at[d], zdev(d))
     send(xg.at[row], xg.at[row], s1x.at[0], r1x.at[0], xl)
     send(xg.at[row], xg.at[row], s1s.at[0], r1s.at[0], sib)
+
+    loads[2].wait()
+    for i, line in enumerate(index_table(slots[...])):
+        tabv[i:i + 1, :K] = line
+    to_scalar = pltpu.make_async_copy(tabv, tab, load_sem.at[7])
+    to_scalar.start()
 
     def from_z(d):
         at = leaf(x, (z + NZ - d) % NZ, k)
@@ -115,26 +136,30 @@
         arrive(xg.at[at], s1x.at[d], r1x.at[d])
         send(xg.at[at], xg.at[at], s1s.at[NZ + d], r1s.at[NZ + d], sib)
 
-    from_z(1), from_z(7), from_x(0), from_z(2), from_z(6), from_x(1), from_x(7)
-    from_z(3), from_z(5), from_x(2), from_x(6), from_z(4), from_x(3), from_x(5), from_x(4)
+    for d in NEAR:
+        from_z(d)
+    for d in (0,) + NEAR:
+        from_x(d)
     for d in (0,) + NEAR:
         arrive(xg.at[leaf(x, (z + NZ - d) % NZ, 1 - k)], s1s.at[d], r1s.at[d])
     for d in (0,) + NEAR:
         arrive(xg.at[leaf(1 - x, (z + NZ - d) % NZ, 1 - k)], s1s.at[NZ + d], r1s.at[NZ + d])
-    load.wait()
+    to_scalar.wait()
+    for i in (3, 4, 5, 6):
+        loads[i].wait()
 
     def forward_turn(turn, total):
         for i in range(8):
             p = turn * 8 + i
-            product = jnp.dot(vals[tab[0, PERM + p]], xg[tab[0, COLP + p]], preferred_element_type=F32)
-            total = total * tab[0, KEEPF + p].astype(F32) + product
+            product = jnp.dot(vals[tab[PERM, p]], xg[tab[COLP, p]], preferred_element_type=F32)
+            total = total * tab[KEEPF, p].astype(F32) + product
             ps[p] = total
         return total
 
     lax.fori_loop(0, K // 8, forward_turn, jnp.zeros((N, N), F32))
 
     def row_sum(at):
-        return ps[tab[0, LASTR + at]] * tab[0, HASR + at].astype(F32)
+        return ps[tab[LASTR, at]] * tab[HASR, at].astype(F32)
 
     for d in FAR + (0,):
         xs2[d] = row_sum((1 - h) * NZ + (y + d) % NZ).astype(BF16)
@@ -168,10 +193,13 @@
         dp = gout[:, cs].astype(F32) * slant
         gwx[c:c + 1, HID:] = jnp.sum(dp, axis=0, keepdims=True)
         dpre[:, cs] = dp.astype(BF16)
+    stores = [pltpu.make_async_copy(here, far, load_sem.at[8 + i]) for i, (here, far) in enumerate(
+        ((act, act_hbm), (gf, gf_hbm), (gw, gw_hbm), (gb, gb_hbm)))]
+    stores[0].start()
     projected = lax.dot_general(w[...], dpre[...], (((1,), (1,)), ((), ())), preferred_element_type=F32)
     bt[col] = (projected * nrow).astype(BF16)
 
-    for d in FAR:
+    for d in MIXED:
         send(bt.at[col], bt.at[col], s4y.at[d], r4y.at[d], ydev(d))
     send(bt.at[col], bt.at[col], s4x.at[0], r4x.at[0], xh)
     gwx[:, :HID] = jnp.dot(scaled.T.astype(BF16), dpre[...], preferred_element_type=F32)
@@ -191,15 +219,15 @@
     def back_turn(turn, total):
         for i in range(8):
             p = turn * 8 + i
-            product = jnp.dot(bt[tab[0, ROWK + p]], vals[p], preferred_element_type=F32)
-            total = total * tab[0, KEEPB + p].astype(F32) + product
+            product = jnp.dot(bt[tab[ROWK, p]], vals[p], preferred_element_type=F32)
+            total = total * tab[KEEPB, p].astype(F32) + product
             ps[p] = total
         return total
 
     lax.fori_loop(0, K // 8, back_turn, jnp.zeros((N, N), F32))
 
     def col_sum(at):
-        return ps[tab[0, LASTC + at]] * tab[0, HASC + at].astype(F32)
+        return ps[tab[LASTC, at]] * tab[HASC, at].astype(F32)
 
     for a in (1, 0):
         xa = 1 - x if a else x
@@ -249,6 +277,7 @@
         arrive(zr5.at[d], s5z.at[d], r5z.at[d])
         back = back + zr5[d].astype(F32)
     gf[...] = (back * nrow).T.astype(BF16)
+    stores[1].start()
     for d in NEAR:
         at = pl.ds(pl.multiple_of((k * NZ + (z + NZ - d) % NZ) * 8, 8), 8)
         arrive(gwo.at[at], sez.at[d], rez.at[d])
@@ -258,34 +287,55 @@
     gw[...] = gwo[:, :HID]
     for c in range(HID // N):
         gb[:, c * N:(c + 1) * N] = gwo[c:c + 1, HID:]
+    stores[2].start()
+    stores[3].start()
     for cp in sent:
         cp.wait_send()
+    for cp in stores:
+        cp.wait()
+
+
+def hand_over(*refs):
+    sources, targets, stops, sems = refs[:4], refs[4:8], refs[8:12], refs[12]
+    ins = [pltpu.make_async_copy(sources[i], stops[i], sems.at[i]) for i in range(4)]
+    outs = [pltpu.make_async_copy(stops[i], targets[i], sems.at[4 + i]) for i in range(4)]
+    for cp in ins:
+        cp.start()
+    for come, go in zip(ins, outs):
+        come.wait()
+        go.start()
+    for cp in outs:
+        cp.wait()
 
 
 def shards(features, degrees, proj_weight, bias, grad_out, tile_slots, tile_values):
-    table = index_table(tile_slots[0, 0]).reshape(1, 256)
-    vmem = pl.BlockSpec(memory_space=pltpu.VMEM)
+    anywhere = pl.BlockSpec(memory_space=pl.ANY)
     sem = pltpu.SemaphoreType.DMA
     tile = lambda *lead: pltpu.VMEM(lead + (N, N), BF16)
     wide = lambda *lead: pltpu.VMEM(lead + (HID + N,), F32)
-    act, gw, gb, gf = pl.pallas_call(
+    shapes = (
+        jax.ShapeDtypeStruct((N, HID), BF16),
+        jax.ShapeDtypeStruct((N, HID), F32),
+        jax.ShapeDtypeStruct((1, HID), F32),
+        jax.ShapeDtypeStruct((N, N), BF16),
+    )
+    outs = pl.pallas_call(
         layer,
         name="layer",
-        out_shape=(
-            jax.ShapeDtypeStruct((N, HID), BF16),
-            jax.ShapeDtypeStruct((N, HID), F32),
-            jax.ShapeDtypeStruct((1, HID), F32),
-            jax.ShapeDtypeStruct((N, N), BF16),
-        ),
-        in_specs=[pl.BlockSpec(memory_space=pltpu.SMEM)] + [vmem] * 5 + [pl.BlockSpec(memory_space=pl.ANY)],
-        out_specs=(vmem,) * 4,
+        out_shape=shapes,
+        in_specs=[anywhere] * 7,
+        out_specs=(anywhere,) * 4,
         scratch_shapes=[
+            *(pltpu.VMEM(shape.shape, shape.dtype) for shape in shapes),
+            pltpu.VMEM((2, K), jnp.int32), pltpu.VMEM((16, N), jnp.int32), pltpu.SMEM((16, N), jnp.int32),
+            tile(), pltpu.VMEM((1, N), jnp.int32), pltpu.VMEM((N, HID), BF16), pltpu.VMEM((1, HID), F32),
+            pltpu.VMEM((N, HID), BF16),
             tile(K), tile(32), pltpu.VMEM((K, N, N), F32),
             tile(8), tile(8), tile(8), tile(8), pltpu.VMEM((N, N), F32),
             pltpu.VMEM((N, HID), BF16), tile(16),
             tile(2, 8), tile(2, 8), tile(8), tile(8), tile(8), tile(8), pltpu.VMEM((N, N), F32),
             wide(N), wide(64), wide(64), wide(8, 8), wide(8, 8), wide(4, 8), wide(N),
-            sem, sem((8,)), sem((8,)), sem((8,)), sem((8,)), sem((16,)), sem((16,)),
+            sem((12,)), sem((8,)), sem((8,)), sem((8,)), sem((8,)), sem((16,)), sem((16,)),
             sem((8,)), sem((8,)), sem((8,)), sem((8,)),
             sem((8,)), sem((8,)), sem((8,)), sem((8,)),
             sem((2,)), sem((2,)), sem((8,)), sem((8,)), sem((8,)), sem((8,)),
@@ -293,9 +343,19 @@
             sem((8,)), sem((8,)), sem, sem,
         ],
         compiler_params=pltpu.CompilerParams(
-            collective_id=0, has_side_effects=True, vmem_limit_bytes=40 << 20),
+            collective_id=0, has_side_effects=True, vmem_limit_bytes=VMEM_LIMIT),
         cost_estimate=pl.CostEstimate(flops=3 * 10 ** 8, bytes_accessed=2 * 10 ** 6, transcendentals=65536),
-    )(table, features, degrees.reshape(1, N), proj_weight, bias.reshape(1, HID), grad_out, tile_values[0, 0])
+    )(tile_slots[0, 0].T, features, degrees.reshape(1, N), proj_weight, bias.reshape(1, HID), grad_out,
+      tile_values[0, 0])
+    act, gw, gb, gf = pl.pallas_call(
+        hand_over,
+        name="hand_over",
+        out_shape=shapes,
+        in_specs=[anywhere] * 4,
+        out_specs=(anywhere,) * 4,
+        scratch_shapes=[pltpu.VMEM(shape.shape, shape.dtype) for shape in shapes] + [sem((8,))],
+        compiler_params=pltpu.CompilerParams(vmem_limit_bytes=VMEM_LIMIT),
+    )(*outs)
     return act, gw, gb.reshape(HID), gf
 
 

time: 92.4 us -> 79.8 us (0.86)
  local copies, waits for them, and re-layouts: 6.32 us -> 0 us
  Pallas kernels: 83 us -> 79 us
  other arithmetic: 2.09 us -> 0 us
    unnamed x16 -> x0, local copies, waits for them, and re-layouts: 6.24 us -> none
    pallas_call x1 -> x2, Pallas kernels: 83 us -> 79 us  [the longest x1 77.2 us: shards(): pl.pallas_call(layer, name='layer', out_shape=shapes, in_specs=[anywhere]...]
where the time goes in v2:
time: 79.8 us; the launch traced here: 79.7 us
  Pallas kernels  79 us (99%)
    pallas_call x1, Pallas kernels, shards(): pl.pallas_call(layer, name='layer', out_shape=shapes, in_specs=[anywhere]...  77.2 us
    pallas_call x1, Pallas kernels, shards(): pl.pallas_call(hand_over, name='hand_over', out_shape=shapes, in_specs=[a...  1.8 us

profile of v2, /device:TPU:1, one launch (start us, length us, event | category | flops | bytes accessed | tf_op | source)
XLA Modules:
  0.0 79.7 jit_solution(9036120125102799818)
XLA Ops:
  0.6 77.2 %layer.1 = (bf16[128,512]{1,0:T(8,128)(2,1)}, f32[128,512]{1,0:T(8,128)}, f32[1,512]{1,0:T(1,128)}, bf16[128,128]{1,0:T(8,128)(2,1)}) custom-call(s32[2,32]{1,0:T(2,128)} %bitcast.9, bf16[128,128]{1,0:T(8,128)(2,1)} %feat_hbm.1, s32[1,128]{1,0:T(1,128)} %bitcast.10, bf16[128,512]{1,0:T(8,128)(2,1)} %w_hbm.1, f32[1,512]{1,0:T(1,128)} %bitcast.8, ...), custom_call_target="tpu_custom_call" | custom-call | flops 300000000 | bytes 2000000 | tf_op jit(solution)/shard_map/layer/pallas_call | solution.py:322
  77.9 1.8 %hand_over.1 = (bf16[128,512]{1,0:T(8,128)(2,1)}, f32[128,512]{1,0:T(8,128)}, f32[1,512]{1,0:T(1,128)}, bf16[128,128]{1,0:T(8,128)(2,1)}) custom-call(bf16[128,512]{1,0:T(8,128)(2,1)} %get-tuple-element.12.refs_0_, f32[128,512]{1,0:T(8,128)} %get-tuple-element.13.refs_1_, f32[1,512]{1,0:T(1,128)} %get-tuple-element.14.refs_2_, ...), custom_call_target="tpu_custom_call" | custom-call | tf_op jit(solution)/shard_map/hand_over/pallas_call | solution.py:350

commit v3 on v2

v3 whole, which is shorter than its diff:
```python
import jax
import jax.numpy as jnp
from jax import lax
from jax.experimental import pallas as pl
from jax.experimental.pallas import tpu as pltpu
from jax.sharding import PartitionSpec as P

MESH = pl.DeviceIdType.MESH
PARTS = 2
VMEM_LIMIT = 57 * 10 ** 6
BF16 = jnp.bfloat16
F32 = jnp.float32

N = 128
HID = 512
K = 32
NZ = 8
FAR = (4, 3, 5, 2, 6, 1, 7)
NEAR = (1, 7, 2, 6, 3, 5, 4)
MIXED = (2, 6, 1, 7, 4, 3, 5)
PERM, COLP, KEEPF, LASTR, HASR, ROWK, KEEPB, LASTC, HASC = range(9)


def index_table(slots):
    rows, cols = slots[0:1, :], slots[1:2, :]
    down = lax.broadcasted_iota(jnp.int32, (K, K), 0)
    along = lax.broadcasted_iota(jnp.int32, (K, K), 1)
    live = rows >= 0
    row_key = jnp.where(live, rows, 16)
    col_key = jnp.where(live, cols, 32)

    def upright(values):
        return jnp.sum(jnp.where(down == along, jnp.broadcast_to(values, (K, K)), 0), axis=1, keepdims=True)

    def place(values, where):
        return jnp.sum(jnp.where(where, jnp.broadcast_to(values, (K, K)), 0), axis=0, keepdims=True)

    def count(where):
        return jnp.sum(where.astype(jnp.int32), axis=0, keepdims=True)

    rows_up, cols_up = upright(row_key), upright(col_key)
    key_up = rows_up * K + down[:, 0:1]
    key = row_key * K + along[0:1, :]
    rank = jnp.sum((jnp.broadcast_to(key, (K, K)) < key_up).astype(jnp.int32), axis=1, keepdims=True)
    here, after = rank == along, rank + 1 == along
    row_here = place(rows_up, here)
    col_here = jnp.minimum(place(cols_up, here), 31)
    spots = (col_here & 1) * 16 + lax.shift_right_logical(col_here, 1)
    return (
        place(down[:, 0:1], here),
        spots,
        (row_here == place(rows_up, after)).astype(jnp.int32),
        jnp.maximum(count(rows_up <= along) - 1, 0),
        (count(rows_up == along) > 0).astype(jnp.int32),
        jnp.minimum(row_key, 15),
        (col_key == place(cols_up, down + 1 == along)).astype(jnp.int32),
        jnp.maximum(count(cols_up <= along) - 1, 0),
        (count(cols_up == along) > 0).astype(jnp.int32),
    )


def layer(slots_hbm, feat_hbm, deg_hbm, w_hbm, bias_hbm, gout_hbm, vals_hbm,
          act_hbm, gw_hbm, gb_hbm, gf_hbm,
          act, gw, gb, gf, slots, tabv, tab, feat, deg, w, bias, gout, vals,
          xg0, xg1, ps, xs2, xr2, ys2, yr2, dpre, bt0, bt1,
          ss5, sr5, xs5, xr5, zs5, zr5,
          gwx, arh_in, arh, zb, yb, xb, gwo,
          load_sem, s1z, r1z, s1x, r1x, s1s, r1s, s2x, r2x, s2y, r2y,
          s4y, r4y, s4x, r4x, s5s, r5s, s5x, r5x, s5z, r5z,
          sa, ra, sbz, rbz, scy, rcy, sdx, rdx, sez, rez, sf, rf):
    row, col = lax.axis_index("row"), lax.axis_index("col")
    x, z, k = row // 16, (row // 2) % NZ, row % 2
    h, y = col // NZ, col % NZ
    xg, bt = (xg0, xg1), (bt0, bt1)
    part = [pl.ds(q * (N // PARTS), N // PARTS) for q in range(PARTS)]

    def leaf(x_, z_, k_):
        return (x_ * NZ + z_) * 2 + k_

    def spot(x_, z_, k_):
        return k_ * 16 + x_ * NZ + z_

    def behind(at, d):
        return (at + NZ - d) % NZ

    def zdev(d):
        return (leaf(x, (z + d) % NZ, k), col)

    def ydev(d):
        return (row, h * NZ + (y + d) % NZ)

    sib = (leaf(x, z, 1 - k), col)
    xl = (leaf(1 - x, z, k), col)
    xh = (row, (1 - h) * NZ + y)
    xlh = (leaf(1 - x, z, k), (1 - h) * NZ + y)

    def copy(src, dst, ssem, rsem, dev):
        return pltpu.make_async_remote_copy(
            src_ref=src, dst_ref=dst, send_sem=ssem, recv_sem=rsem, device_id=dev, device_id_type=MESH)

    sent = []

    def send(src, dst, ssem, rsem, dev):
        cp = copy(src, dst, ssem, rsem, dev)
        cp.start()
        sent.append(cp)

    def arrive(dst, ssem, rsem):
        copy(dst, dst, ssem, rsem, sib).wait_recv()

    barrier = pltpu.get_barrier_semaphore()
    partners = [sib, xl, xh, xlh] + [zdev(d) for d in NEAR] + [ydev(d) for d in NEAR]
    for dev in partners:
        pl.semaphore_signal(barrier, inc=1, device_id=dev, device_id_type=MESH)
    loads = []
    for i, (far, here) in enumerate((
            (deg_hbm, deg), (feat_hbm, feat), (slots_hbm, slots), (vals_hbm, vals), (w_hbm, w), (bias_hbm, bias),
            (gout_hbm, gout))):
        loads.append(pltpu.make_async_copy(far, here, load_sem.at[i]))
        loads[i].start()
    stores = [pltpu.make_async_copy(here, far, load_sem.at[8 + i]) for i, (here, far) in enumerate(
        ((act, act_hbm), (gf, gf_hbm), (gw, gw_hbm), (gb, gb_hbm)))]
    loads[0].wait()
    loads[1].wait()

    nrow = lax.rsqrt(deg[...].astype(F32))
    mine = spot(x, z, k)
    scaled = (feat[...].astype(F32).T * nrow).astype(BF16)
    for q in range(PARTS):
        xg[q][mine] = scaled[q * (N // PARTS):(q + 1) * (N // PARTS)]
    pl.semaphore_wait(barrier, len(partners))

    for q in range(PARTS):
        at = xg[q].at[mine]
        for d in MIXED:
            send(at, at, s1z.at[q, d], r1z.at[q, d], zdev(d))
        send(at, at, s1x.at[q, 0], r1x.at[q, 0], xl)

    loads[2].wait()
    for i, line in enumerate(index_table(slots[...])):
        tabv[i:i + 1, :K] = line
    to_scalar = pltpu.make_async_copy(tabv, tab, load_sem.at[7])
    to_scalar.start()

    def half_to_sib(q, i, x_):
        at = xg[q].at[pl.ds(spot(x_, 0, k), NZ)]
        send(at, at, s1s.at[q, i], r1s.at[q, i], sib)

    def half_from_sib(q, i, x_):
        arrive(xg[q].at[pl.ds(spot(x_, 0, 1 - k), NZ)], s1s.at[q, i], r1s.at[q, i])

    for q in range(PARTS):
        for d in NEAR:
            at = xg[q].at[spot(x, behind(z, d), k)]
            arrive(at, s1z.at[q, d], r1z.at[q, d])
            send(at, at, s1x.at[q, d], r1x.at[q, d], xl)
        half_to_sib(q, 0, x)
    to_scalar.wait()
    loads[3].wait()

    def row_sum(at, q):
        return ps[tab[LASTR, at], part[q]] * tab[HASR, at].astype(F32)

    for q in range(PARTS):
        for d in (0,) + NEAR:
            arrive(xg[q].at[spot(1 - x, behind(z, d), k)], s1x.at[q, d], r1x.at[q, d])
        half_to_sib(q, 1, 1 - x)
        half_from_sib(q, 0, x)
        half_from_sib(q, 1, 1 - x)

        def forward_turn(turn, total):
            for i in range(8):
                p = turn * 8 + i
                product = lax.dot_general(xg[q][tab[COLP, p]], vals[tab[PERM, p]],
                                          (((1,), (1,)), ((), ())), preferred_element_type=F32)
                total = total * tab[KEEPF, p].astype(F32) + product
                ps[p, part[q]] = total
            return total

        lax.fori_loop(0, K // 8, forward_turn, jnp.zeros((N // PARTS, N), F32))
        for d in FAR + (0,):
            xs2[d, part[q]] = row_sum((1 - h) * NZ + (y + d) % NZ, q).astype(BF16)
            send(xs2.at[d, part[q]], xr2.at[d, part[q]], s2x.at[q, d], r2x.at[q, d], xh)
    smooth = [None] * PARTS
    for q in range(PARTS):
        for d in FAR + (0,):
            own = row_sum(h * NZ + (y + d) % NZ, q)
            arrive(xr2.at[d, part[q]], s2x.at[q, d], r2x.at[q, d])
            both = own + xr2[d, part[q]].astype(F32)
            if d:
                ys2[d, part[q]] = both.astype(BF16)
                send(ys2.at[d, part[q]], yr2.at[d, part[q]], s2y.at[q, d], r2y.at[q, d], ydev(d))
            else:
                smooth[q] = both
    for i in (4, 5, 6):
        loads[i].wait()
    for q in range(PARTS):
        for d in NEAR:
            arrive(yr2.at[d, part[q]], s2y.at[q, d], r2y.at[q, d])
            smooth[q] = smooth[q] + yr2[d, part[q]].astype(F32)

    smoothed = (jnp.concatenate(smooth, axis=0) * nrow).astype(BF16)
    gwx[...] = jnp.zeros((N, HID + N), F32)
    for c in range(HID // N):
        cs = slice(c * N, (c + 1) * N)
        pre = lax.dot_general(smoothed, w[:, cs], (((0,), (0,)), ((), ())), preferred_element_type=F32) + bias[:, cs]
        square = pre * pre
        slope = 0.7978845608028654
        t = jnp.tanh(slope * (pre + 0.044715 * (square * pre)))
        half = 0.5 * (1.0 + t)
        act[:, cs] = (pre * half).astype(BF16)
        slant = half + (0.5 * slope) * pre * (1.0 - t * t) * (1.0 + (3 * 0.044715) * square)
        dp = gout[:, cs].astype(F32) * slant
        gwx[c:c + 1, HID:] = jnp.sum(dp, axis=0, keepdims=True)
        dpre[:, cs] = dp.astype(BF16)
    projected = lax.dot_general(w[...], dpre[...], (((1,), (1,)), ((), ())), preferred_element_type=F32)
    back_in = (projected * nrow).astype(BF16)
    for q in range(PARTS):
        bt[q][col] = back_in[q * (N // PARTS):(q + 1) * (N // PARTS)]

    for q in range(PARTS):
        at = bt[q].at[col]
        for d in MIXED:
            send(at, at, s4y.at[q, d], r4y.at[q, d], ydev(d))
        send(at, at, s4x.at[q, 0], r4x.at[q, 0], xh)
    stores[0].start()
    gwx[:, :HID] = jnp.dot(smoothed, dpre[...], preferred_element_type=F32)
    ours, theirs = pl.ds(pl.multiple_of(k * 64, 64), 64), pl.ds(pl.multiple_of((1 - k) * 64, 64), 64)
    send(gwx.at[theirs], arh_in, sa, ra, sib)
    arrive(arh_in, sa, ra)
    arh[...] = gwx[ours] + arh_in[...]
    for d in FAR:
        at = pl.multiple_of(((z + d) % NZ) * 8, 8)
        send(arh.at[pl.ds(at, 8)], zb.at[d], sbz.at[d], rbz.at[d], zdev(d))
    for q in range(PARTS):
        for d in NEAR:
            at = bt[q].at[h * NZ + behind(y, d)]
            arrive(at, s4y.at[q, d], r4y.at[q, d])
            send(at, at, s4x.at[q, d], r4x.at[q, d], xh)
    chunk = arh[pl.ds(pl.multiple_of(z * 8, 8), 8)]
    for d in NEAR:
        arrive(zb.at[d], sbz.at[d], rbz.at[d])
        chunk = chunk + zb[d]
    yb[y] = chunk
    for d in FAR:
        send(yb.at[y], yb.at[y], scy.at[d], rcy.at[d], ydev(d))

    def col_sum(at, q):
        return ps[tab[LASTC, at], part[q]] * tab[HASC, at].astype(F32)

    def to_x(q):
        arrive(sr5.at[1, :, part[q]], s5s.at[q, 1], r5s.at[q, 1])
        for d in FAR + (0,):
            xs5[d, part[q]] = (col_sum(leaf(1 - x, (z + d) % NZ, k), q) + sr5[1, d, part[q]].astype(F32)).astype(BF16)
            send(xs5.at[d, part[q]], xr5.at[d, part[q]], s5x.at[q, d], r5x.at[q, d], xl)

    for q in range(PARTS):
        for d in (0,) + NEAR:
            arrive(bt[q].at[(1 - h) * NZ + behind(y, d)], s4x.at[q, d], r4x.at[q, d])
        if q:
            to_x(q - 1)

        def back_turn(turn, total):
            for i in range(8):
                p = turn * 8 + i
                product = jnp.dot(bt[q][tab[ROWK, p]], vals[p], preferred_element_type=F32)
                total = total * tab[KEEPB, p].astype(F32) + product
                ps[p, part[q]] = total
            return total

        lax.fori_loop(0, K // 8, back_turn, jnp.zeros((N // PARTS, N), F32))
        for a in (1, 0):
            xa = 1 - x if a else x
            for d in range(NZ):
                ss5[a, d, part[q]] = col_sum(leaf(xa, (z + d) % NZ, 1 - k), q).astype(BF16)
            send(ss5.at[a, :, part[q]], sr5.at[a, :, part[q]], s5s.at[q, a], r5s.at[q, a], sib)
    to_x(PARTS - 1)
    for d in NEAR:
        arrive(yb.at[behind(y, d)], scy.at[d], rcy.at[d])
    chunk = yb[0]
    for i in range(1, NZ):
        chunk = chunk + yb[i]
    me = x * 2 + h
    xb[me] = chunk
    send(xb.at[me], xb.at[me], sdx.at[0], rdx.at[0], xl)
    send(xb.at[me], xb.at[me], sdx.at[1], rdx.at[1], xh)
    send(xb.at[me], xb.at[me], sdx.at[2], rdx.at[2], xlh)
    back = [None] * PARTS
    for q in range(PARTS):
        arrive(sr5.at[0, :, part[q]], s5s.at[q, 0], r5s.at[q, 0])
        for d in FAR + (0,):
            own = col_sum(leaf(x, (z + d) % NZ, k), q) + sr5[0, d, part[q]].astype(F32)
            arrive(xr5.at[d, part[q]], s5x.at[q, d], r5x.at[q, d])
            both = own + xr5[d, part[q]].astype(F32)
            if d:
                zs5[d, part[q]] = both.astype(BF16)
                send(zs5.at[d, part[q]], zr5.at[d, part[q]], s5z.at[q, d], r5z.at[q, d], zdev(d))
            else:
                back[q] = both
    arrive(xb.at[(1 - x) * 2 + h], sdx.at[0], rdx.at[0])
    arrive(xb.at[x * 2 + 1 - h], sdx.at[1], rdx.at[1])
    arrive(xb.at[(1 - x) * 2 + 1 - h], sdx.at[2], rdx.at[2])
    rows = pl.ds(pl.multiple_of((k * NZ + z) * 8, 8), 8)
    gwo[rows] = ((xb[0] + xb[1]) + (xb[2] + xb[3])) * (65536.0 ** -0.5)
    for d in FAR:
        send(gwo.at[rows], gwo.at[rows], sez.at[d], rez.at[d], zdev(d))
    for q in range(PARTS):
        for d in NEAR:
            arrive(zr5.at[d, part[q]], s5z.at[q, d], r5z.at[q, d])
            back[q] = back[q] + zr5[d, part[q]].astype(F32)
    gf[...] = (jnp.concatenate(back, axis=0) * nrow).T.astype(BF16)
    stores[1].start()
    for d in NEAR:
        at = pl.ds(pl.multiple_of((k * NZ + behind(z, d)) * 8, 8), 8)
        arrive(gwo.at[at], sez.at[d], rez.at[d])
    send(gwo.at[ours], gwo.at[ours], sf, rf, sib)
    arrive(gwo.at[theirs], sf, rf)
    gw[...] = gwo[:, :HID]
    for c in range(HID // N):
        gb[:, c * N:(c + 1) * N] = gwo[c:c + 1, HID:]
    stores[2].start()
    stores[3].start()
    for cp in sent:
        cp.wait_send()
    for cp in stores:
        cp.wait()


def hand_over(*refs):
    sources, targets, stops, sems = refs[:4], refs[4:8], refs[8:12], refs[12]
    ins = [pltpu.make_async_copy(sources[i], stops[i], sems.at[i]) for i in range(4)]
    outs = [pltpu.make_async_copy(stops[i], targets[i], sems.at[4 + i]) for i in range(4)]
    for cp in ins:
        cp.start()
    for come, go in zip(ins, outs):
        come.wait()
        go.start()
    for cp in outs:
        cp.wait()


def shards(features, degrees, proj_weight, bias, grad_out, tile_slots, tile_values):
    anywhere = pl.BlockSpec(memory_space=pl.ANY)
    sem = pltpu.SemaphoreType.DMA
    tile = lambda *lead: pltpu.VMEM(lead + (N, N), BF16)
    flat = lambda count: pltpu.VMEM((count, N // PARTS, N), BF16)
    wide = lambda *lead: pltpu.VMEM(lead + (HID + N,), F32)
    shapes = (
        jax.ShapeDtypeStruct((N, HID), BF16),
        jax.ShapeDtypeStruct((N, HID), F32),
        jax.ShapeDtypeStruct((1, HID), F32),
        jax.ShapeDtypeStruct((N, N), BF16),
    )
    outs = pl.pallas_call(
        layer,
        name="layer",
        out_shape=shapes,
        in_specs=[anywhere] * 7,
        out_specs=(anywhere,) * 4,
        scratch_shapes=[
            *(pltpu.VMEM(shape.shape, shape.dtype) for shape in shapes),
            pltpu.VMEM((2, K), jnp.int32), pltpu.VMEM((16, N), jnp.int32), pltpu.SMEM((16, N), jnp.int32),
            tile(), pltpu.VMEM((1, N), jnp.int32), pltpu.VMEM((N, HID), BF16), pltpu.VMEM((1, HID), F32),
            pltpu.VMEM((N, HID), BF16),
            tile(K), flat(32), flat(32), pltpu.VMEM((K, N, N), F32),
            tile(8), tile(8), tile(8), tile(8), pltpu.VMEM((N, HID), BF16), flat(16), flat(16),
            tile(2, 8), tile(2, 8), tile(8), tile(8), tile(8), tile(8),
            wide(N), wide(64), wide(64), wide(8, 8), wide(8, 8), wide(4, 8), wide(N),
            sem((12,)), *[sem((PARTS, 8))] * 4, *[sem((PARTS, 2))] * 2, *[sem((PARTS, 8))] * 8,
            *[sem((PARTS, 2))] * 2, *[sem((PARTS, 8))] * 4,
            sem, sem, sem((8,)), sem((8,)), sem((8,)), sem((8,)), sem((3,)), sem((3,)),
            sem((8,)), sem((8,)), sem, sem,
        ],
        compiler_params=pltpu.CompilerParams(
            collective_id=0, has_side_effects=True, vmem_limit_bytes=VMEM_LIMIT),
        cost_estimate=pl.CostEstimate(flops=3 * 10 ** 8, bytes_accessed=2 * 10 ** 6, transcendentals=65536),
    )(tile_slots[0, 0].T, features, degrees.reshape(1, N), proj_weight, bias.reshape(1, HID), grad_out,
      tile_values[0, 0])
    act, gw, gb, gf = pl.pallas_call(
        hand_over,
        name="hand_over",
        out_shape=shapes,
        in_specs=[anywhere] * 4,
        out_specs=(anywhere,) * 4,
        scratch_shapes=[pltpu.VMEM(shape.shape, shape.dtype) for shape in shapes] + [sem((8,))],
        compiler_params=pltpu.CompilerParams(vmem_limit_bytes=VMEM_LIMIT),
    )(*outs)
    return act, gw, gb.reshape(HID), gf


def solution(mesh):
    leaf = P(("row", "col"))
    leaf_rows = P(("row", "col"), None)
    return jax.shard_map(
        shards,
        mesh=mesh,
        in_specs=(leaf_rows, leaf, P(), P(), leaf_rows, P("row", "col", None, None), P("row", "col", None, None, None)),
        out_specs=(leaf_rows, P(), P(), leaf_rows),
        check_vma=False,
    )
```

time: 79.8 us -> 74.5 us (0.934)
  Pallas kernels: 79 us -> 73.7 us
    pallas_call x1, Pallas kernels: 77.2 us -> 71.9 us  [shards(): pl.pallas_call(layer, name='layer', out_shape=shapes, in_specs=[anywhere]...]
where the time goes in v3:
time: 74.5 us; the launch traced here: 74.3 us
  Pallas kernels  73.7 us (99%)
    pallas_call x1, Pallas kernels, shards(): pl.pallas_call(layer, name='layer', out_shape=shapes, in_specs=[anywhere]...  71.9 us
    pallas_call x1, Pallas kernels, shards(): pl.pallas_call(hand_over, name='hand_over', out_shape=shapes, in_specs=[a...  1.8 us

profile of v3, /device:TPU:1, one launch (start us, length us, event | category | flops | bytes accessed | tf_op | source)
XLA Modules:
  0.0 74.3 jit_solution(8305221793178166087)
XLA Ops:
  0.6 71.9 %layer.1 = (bf16[128,512]{1,0:T(8,128)(2,1)}, f32[128,512]{1,0:T(8,128)}, f32[1,512]{1,0:T(1,128)}, bf16[128,128]{1,0:T(8,128)(2,1)}) custom-call(s32[2,32]{1,0:T(2,128)} %bitcast.9, bf16[128,128]{1,0:T(8,128)(2,1)} %feat_hbm.1, s32[1,128]{1,0:T(1,128)} %bitcast.10, bf16[128,512]{1,0:T(8,128)(2,1)} %w_hbm.1, f32[1,512]{1,0:T(1,128)} %bitcast.8, ...), custom_call_target="tpu_custom_call" | custom-call | flops 300000000 | bytes 2000000 | tf_op jit(solution)/shard_map/layer/pallas_call | solution.py:354
  72.5 1.8 %hand_over.1 = (bf16[128,512]{1,0:T(8,128)(2,1)}, f32[128,512]{1,0:T(8,128)}, f32[1,512]{1,0:T(1,128)}, bf16[128,128]{1,0:T(8,128)(2,1)}) custom-call(bf16[128,512]{1,0:T(8,128)(2,1)} %get-tuple-element.12.refs_0_, f32[128,512]{1,0:T(8,128)} %get-tuple-element.13.refs_1_, f32[1,512]{1,0:T(1,128)} %get-tuple-element.14.refs_2_, ...), custom_call_target="tpu_custom_call" | custom-call | tf_op jit(solution)/shard_map/hand_over/pallas_call | solution.py:379

commit v4 on v3

--- a/solution.py
+++ b/solution.py
@@ -13,6 +13,7 @@
 
 N = 128
 HID = 512
+WIDE = HID // 2 + N
 K = 32
 NZ = 8
 FAR = (4, 3, 5, 2, 6, 1, 7)
@@ -64,7 +65,7 @@
           act, gw, gb, gf, slots, tabv, tab, feat, deg, w, bias, gout, vals,
           xg0, xg1, ps, xs2, xr2, ys2, yr2, dpre, bt0, bt1,
           ss5, sr5, xs5, xr5, zs5, zr5,
-          gwx, arh_in, arh, zb, yb, xb, gwo,
+          gwx, arh_in, arh, zs, zb, yb, xb, gwo,
           load_sem, s1z, r1z, s1x, r1x, s1s, r1s, s2x, r2x, s2y, r2y,
           s4y, r4y, s4x, r4x, s5s, r5s, s5x, r5x, s5z, r5z,
           sa, ra, sbz, rbz, scy, rcy, sdx, rdx, sez, rez, sf, rf):
@@ -98,12 +99,16 @@
         return pltpu.make_async_remote_copy(
             src_ref=src, dst_ref=dst, send_sem=ssem, recv_sem=rsem, device_id=dev, device_id_type=MESH)
 
-    sent = []
-
-    def send(src, dst, ssem, rsem, dev):
+    sent = {1: [], 2: [], 4: [], 5: []}
+
+    def send(phase, src, dst, ssem, rsem, dev):
         cp = copy(src, dst, ssem, rsem, dev)
         cp.start()
-        sent.append(cp)
+        sent[phase].append(cp)
+
+    def settle(phase):
+        for cp in sent[phase]:
+            cp.wait_send()
 
     def arrive(dst, ssem, rsem):
         copy(dst, dst, ssem, rsem, sib).wait_recv()
@@ -133,8 +138,8 @@
     for q in range(PARTS):
         at = xg[q].at[mine]
         for d in MIXED:
-            send(at, at, s1z.at[q, d], r1z.at[q, d], zdev(d))
-        send(at, at, s1x.at[q, 0], r1x.at[q, 0], xl)
+            send(1, at, at, s1z.at[q, d], r1z.at[q, d], zdev(d))
+        send(1, at, at, s1x.at[q, 0], r1x.at[q, 0], xl)
 
     loads[2].wait()
     for i, line in enumerate(index_table(slots[...])):
@@ -144,7 +149,7 @@
 
     def half_to_sib(q, i, x_):
         at = xg[q].at[pl.ds(spot(x_, 0, k), NZ)]
-        send(at, at, s1s.at[q, i], r1s.at[q, i], sib)
+        send(1, at, at, s1s.at[q, i], r1s.at[q, i], sib)
 
     def half_from_sib(q, i, x_):
         arrive(xg[q].at[pl.ds(spot(x_, 0, 1 - k), NZ)], s1s.at[q, i], r1s.at[q, i])
@@ -153,7 +158,7 @@
         for d in NEAR:
             at = xg[q].at[spot(x, behind(z, d), k)]
             arrive(at, s1z.at[q, d], r1z.at[q, d])
-            send(at, at, s1x.at[q, d], r1x.at[q, d], xl)
+            send(1, at, at, s1x.at[q, d], r1x.at[q, d], xl)
         half_to_sib(q, 0, x)
     to_scalar.wait()
     loads[3].wait()
@@ -180,7 +185,8 @@
         lax.fori_loop(0, K // 8, forward_turn, jnp.zeros((N // PARTS, N), F32))
         for d in FAR + (0,):
             xs2[d, part[q]] = row_sum((1 - h) * NZ + (y + d) % NZ, q).astype(BF16)
-            send(xs2.at[d, part[q]], xr2.at[d, part[q]], s2x.at[q, d], r2x.at[q, d], xh)
+            send(2, xs2.at[d, part[q]], xr2.at[d, part[q]], s2x.at[q, d], r2x.at[q, d], xh)
+    settle(1)
     smooth = [None] * PARTS
     for q in range(PARTS):
         for d in FAR + (0,):
@@ -189,7 +195,7 @@
             both = own + xr2[d, part[q]].astype(F32)
             if d:
                 ys2[d, part[q]] = both.astype(BF16)
-                send(ys2.at[d, part[q]], yr2.at[d, part[q]], s2y.at[q, d], r2y.at[q, d], ydev(d))
+                send(2, ys2.at[d, part[q]], yr2.at[d, part[q]], s2y.at[q, d], r2y.at[q, d], ydev(d))
             else:
                 smooth[q] = both
     for i in (4, 5, 6):
@@ -200,7 +206,7 @@
             smooth[q] = smooth[q] + yr2[d, part[q]].astype(F32)
 
     smoothed = (jnp.concatenate(smooth, axis=0) * nrow).astype(BF16)
-    gwx[...] = jnp.zeros((N, HID + N), F32)
+    gwx[...] = jnp.zeros((2, N, WIDE), F32)
     for c in range(HID // N):
         cs = slice(c * N, (c + 1) * N)
         pre = lax.dot_general(smoothed, w[:, cs], (((0,), (0,)), ((), ())), preferred_element_type=F32) + bias[:, cs]
@@ -211,7 +217,7 @@
         act[:, cs] = (pre * half).astype(BF16)
         slant = half + (0.5 * slope) * pre * (1.0 - t * t) * (1.0 + (3 * 0.044715) * square)
         dp = gout[:, cs].astype(F32) * slant
-        gwx[c:c + 1, HID:] = jnp.sum(dp, axis=0, keepdims=True)
+        gwx[c // 2, c % 2:c % 2 + 1, HID // 2:] = jnp.sum(dp, axis=0, keepdims=True)
         dpre[:, cs] = dp.astype(BF16)
     projected = lax.dot_general(w[...], dpre[...], (((1,), (1,)), ((), ())), preferred_element_type=F32)
     back_in = (projected * nrow).astype(BF16)
@@ -221,29 +227,36 @@
     for q in range(PARTS):
         at = bt[q].at[col]
         for d in MIXED:
-            send(at, at, s4y.at[q, d], r4y.at[q, d], ydev(d))
-        send(at, at, s4x.at[q, 0], r4x.at[q, 0], xh)
+            send(4, at, at, s4y.at[q, d], r4y.at[q, d], ydev(d))
+        send(4, at, at, s4x.at[q, 0], r4x.at[q, 0], xh)
     stores[0].start()
-    gwx[:, :HID] = jnp.dot(smoothed, dpre[...], preferred_element_type=F32)
+    for i in range(2):
+        cs = slice(i * HID // 2, (i + 1) * HID // 2)
+        gwx[i, :, :HID // 2] = jnp.dot(smoothed, dpre[:, cs], preferred_element_type=F32)
     ours, theirs = pl.ds(pl.multiple_of(k * 64, 64), 64), pl.ds(pl.multiple_of((1 - k) * 64, 64), 64)
-    send(gwx.at[theirs], arh_in, sa, ra, sib)
+    send(4, gwx.at[:, theirs], arh_in, sa, ra, sib)
     arrive(arh_in, sa, ra)
-    arh[...] = gwx[ours] + arh_in[...]
+    arh[...] = gwx[:, ours] + arh_in[...]
+
+    def eighth(at):
+        return arh[at % 2, pl.ds(pl.multiple_of(at // 2 * 16, 16), 16)]
+
     for d in FAR:
-        at = pl.multiple_of(((z + d) % NZ) * 8, 8)
-        send(arh.at[pl.ds(at, 8)], zb.at[d], sbz.at[d], rbz.at[d], zdev(d))
+        zs[d] = eighth((z + d) % NZ).astype(BF16)
+        send(4, zs.at[d], zb.at[d], sbz.at[d], rbz.at[d], zdev(d))
+    settle(2)
     for q in range(PARTS):
         for d in NEAR:
             at = bt[q].at[h * NZ + behind(y, d)]
             arrive(at, s4y.at[q, d], r4y.at[q, d])
-            send(at, at, s4x.at[q, d], r4x.at[q, d], xh)
-    chunk = arh[pl.ds(pl.multiple_of(z * 8, 8), 8)]
+            send(4, at, at, s4x.at[q, d], r4x.at[q, d], xh)
+    chunk = eighth(z)
     for d in NEAR:
         arrive(zb.at[d], sbz.at[d], rbz.at[d])
-        chunk = chunk + zb[d]
-    yb[y] = chunk
+        chunk = chunk + zb[d].astype(F32)
+    yb[y] = chunk.astype(BF16)
     for d in FAR:
-        send(yb.at[y], yb.at[y], scy.at[d], rcy.at[d], ydev(d))
+        send(4, yb.at[y], yb.at[y], scy.at[d], rcy.at[d], ydev(d))
 
     def col_sum(at, q):
         return ps[tab[LASTC, at], part[q]] * tab[HASC, at].astype(F32)
@@ -252,7 +265,7 @@
         arrive(sr5.at[1, :, part[q]], s5s.at[q, 1], r5s.at[q, 1])
         for d in FAR + (0,):
             xs5[d, part[q]] = (col_sum(leaf(1 - x, (z + d) % NZ, k), q) + sr5[1, d, part[q]].astype(F32)).astype(BF16)
-            send(xs5.at[d, part[q]], xr5.at[d, part[q]], s5x.at[q, d], r5x.at[q, d], xl)
+            send(5, xs5.at[d, part[q]], xr5.at[d, part[q]], s5x.at[q, d], r5x.at[q, d], xl)
 
     for q in range(PARTS):
         for d in (0,) + NEAR:
@@ -273,18 +286,19 @@
             xa = 1 - x if a else x
             for d in range(NZ):
                 ss5[a, d, part[q]] = col_sum(leaf(xa, (z + d) % NZ, 1 - k), q).astype(BF16)
-            send(ss5.at[a, :, part[q]], sr5.at[a, :, part[q]], s5s.at[q, a], r5s.at[q, a], sib)
-    to_x(PARTS - 1)
+            send(5, ss5.at[a, :, part[q]], sr5.at[a, :, part[q]], s5s.at[q, a], r5s.at[q, a], sib)
     for d in NEAR:
         arrive(yb.at[behind(y, d)], scy.at[d], rcy.at[d])
-    chunk = yb[0]
+    chunk = yb[0].astype(F32)
     for i in range(1, NZ):
-        chunk = chunk + yb[i]
+        chunk = chunk + yb[i].astype(F32)
     me = x * 2 + h
     xb[me] = chunk
-    send(xb.at[me], xb.at[me], sdx.at[0], rdx.at[0], xl)
-    send(xb.at[me], xb.at[me], sdx.at[1], rdx.at[1], xh)
-    send(xb.at[me], xb.at[me], sdx.at[2], rdx.at[2], xlh)
+    send(5, xb.at[me], xb.at[me], sdx.at[0], rdx.at[0], xl)
+    send(5, xb.at[me], xb.at[me], sdx.at[1], rdx.at[1], xh)
+    send(5, xb.at[me], xb.at[me], sdx.at[2], rdx.at[2], xlh)
+    to_x(PARTS - 1)
+    settle(4)
     back = [None] * PARTS
     for q in range(PARTS):
         arrive(sr5.at[0, :, part[q]], s5s.at[q, 0], r5s.at[q, 0])
@@ -294,34 +308,34 @@
             both = own + xr5[d, part[q]].astype(F32)
             if d:
                 zs5[d, part[q]] = both.astype(BF16)
-                send(zs5.at[d, part[q]], zr5.at[d, part[q]], s5z.at[q, d], r5z.at[q, d], zdev(d))
+                send(5, zs5.at[d, part[q]], zr5.at[d, part[q]], s5z.at[q, d], r5z.at[q, d], zdev(d))
             else:
                 back[q] = both
-    arrive(xb.at[(1 - x) * 2 + h], sdx.at[0], rdx.at[0])
-    arrive(xb.at[x * 2 + 1 - h], sdx.at[1], rdx.at[1])
-    arrive(xb.at[(1 - x) * 2 + 1 - h], sdx.at[2], rdx.at[2])
-    rows = pl.ds(pl.multiple_of((k * NZ + z) * 8, 8), 8)
-    gwo[rows] = ((xb[0] + xb[1]) + (xb[2] + xb[3])) * (65536.0 ** -0.5)
-    for d in FAR:
-        send(gwo.at[rows], gwo.at[rows], sez.at[d], rez.at[d], zdev(d))
+        if q == 0:
+            arrive(xb.at[(1 - x) * 2 + h], sdx.at[0], rdx.at[0])
+            arrive(xb.at[x * 2 + 1 - h], sdx.at[1], rdx.at[1])
+            arrive(xb.at[(1 - x) * 2 + 1 - h], sdx.at[2], rdx.at[2])
+            gwo[k * NZ + z] = (((xb[0] + xb[1]) + (xb[2] + xb[3])) * (65536.0 ** -0.5)).astype(BF16)
+            for d in FAR:
+                send(5, gwo.at[k * NZ + z], gwo.at[k * NZ + z], sez.at[d], rez.at[d], zdev(d))
+    for d in NEAR:
+        arrive(gwo.at[k * NZ + behind(z, d)], sez.at[d], rez.at[d])
+    send(5, gwo.at[pl.ds(k * NZ, NZ)], gwo.at[pl.ds(k * NZ, NZ)], sf, rf, sib)
     for q in range(PARTS):
         for d in NEAR:
             arrive(zr5.at[d, part[q]], s5z.at[q, d], r5z.at[q, d])
             back[q] = back[q] + zr5[d, part[q]].astype(F32)
     gf[...] = (jnp.concatenate(back, axis=0) * nrow).T.astype(BF16)
     stores[1].start()
-    for d in NEAR:
-        at = pl.ds(pl.multiple_of((k * NZ + behind(z, d)) * 8, 8), 8)
-        arrive(gwo.at[at], sez.at[d], rez.at[d])
-    send(gwo.at[ours], gwo.at[ours], sf, rf, sib)
-    arrive(gwo.at[theirs], sf, rf)
-    gw[...] = gwo[:, :HID]
+    arrive(gwo.at[pl.ds((1 - k) * NZ, NZ)], sf, rf)
+    for i in range(16):
+        rows, cs = slice(i // 2 * 16, i // 2 * 16 + 16), slice(i % 2 * HID // 2, (i % 2 + 1) * HID // 2)
+        gw[rows, cs] = gwo[i, :, :HID // 2].astype(F32)
     for c in range(HID // N):
-        gb[:, c * N:(c + 1) * N] = gwo[c:c + 1, HID:]
+        gb[:, c * N:(c + 1) * N] = gwo[c // 2, :, HID // 2:].astype(F32)[c % 2:c % 2 + 1]
     stores[2].start()
     stores[3].start()
-    for cp in sent:
-        cp.wait_send()
+    settle(5)
     for cp in stores:
         cp.wait()
 
@@ -344,7 +358,7 @@
     sem = pltpu.SemaphoreType.DMA
     tile = lambda *lead: pltpu.VMEM(lead + (N, N), BF16)
     flat = lambda count: pltpu.VMEM((count, N // PARTS, N), BF16)
-    wide = lambda *lead: pltpu.VMEM(lead + (HID + N,), F32)
+    wide = lambda kind, *lead: pltpu.VMEM(lead + (WIDE,), kind)
     shapes = (
         jax.ShapeDtypeStruct((N, HID), BF16),
         jax.ShapeDtypeStruct((N, HID), F32),
@@ -365,7 +379,8 @@
             tile(K), flat(32), flat(32), pltpu.VMEM((K, N, N), F32),
             tile(8), tile(8), tile(8), tile(8), pltpu.VMEM((N, HID), BF16), flat(16), flat(16),
             tile(2, 8), tile(2, 8), tile(8), tile(8), tile(8), tile(8),
-            wide(N), wide(64), wide(64), wide(8, 8), wide(8, 8), wide(4, 8), wide(N),
+            wide(F32, 2, N), wide(F32, 2, 64), wide(F32, 2, 64), wide(BF16, 8, 16), wide(BF16, 8, 16), wide(BF16, 8, 16),
+            wide(F32, 4, 16), wide(BF16, 16, 16),
             sem((12,)), *[sem((PARTS, 8))] * 4, *[sem((PARTS, 2))] * 2, *[sem((PARTS, 8))] * 8,
             *[sem((PARTS, 2))] * 2, *[sem((PARTS, 8))] * 4,
             sem, sem, sem((8,)), sem((8,)), sem((8,)), sem((8,)), sem((3,)), sem((3,)),

time: 74.5 us -> 72.4 us (0.972)
  Pallas kernels: 73.7 us -> 71.6 us
    pallas_call x1, Pallas kernels: 71.9 us -> 69.8 us  [shards(): pl.pallas_call(layer, name='layer', out_shape=shapes, in_specs=[anywhere]...]
where the time goes in v4:
time: 72.4 us; the launch traced here: 72.3 us
  Pallas kernels  71.6 us (99%)
    pallas_call x1, Pallas kernels, shards(): pl.pallas_call(layer, name='layer', out_shape=shapes, in_specs=[anywhere]...  69.8 us
    pallas_call x1, Pallas kernels, shards(): pl.pallas_call(hand_over, name='hand_over', out_shape=shapes, in_specs=[a...  1.8 us

profile of v4, /device:TPU:1, one launch (start us, length us, event | category | flops | bytes accessed | tf_op | source)
XLA Modules:
  0.0 72.3 jit_solution(2796189171212279622)
XLA Ops:
  0.6 69.8 %layer.1 = (bf16[128,512]{1,0:T(8,128)(2,1)}, f32[128,512]{1,0:T(8,128)}, f32[1,512]{1,0:T(1,128)}, bf16[128,128]{1,0:T(8,128)(2,1)}) custom-call(s32[2,32]{1,0:T(2,128)} %bitcast.9, bf16[128,128]{1,0:T(8,128)(2,1)} %feat_hbm.1, s32[1,128]{1,0:T(1,128)} %bitcast.10, bf16[128,512]{1,0:T(8,128)(2,1)} %w_hbm.1, f32[1,512]{1,0:T(1,128)} %bitcast.8, ...), custom_call_target="tpu_custom_call" | custom-call | flops 300000000 | bytes 2000000 | tf_op jit(solution)/shard_map/layer/pallas_call | solution.py:368
  70.5 1.8 %hand_over.1 = (bf16[128,512]{1,0:T(8,128)(2,1)}, f32[128,512]{1,0:T(8,128)}, f32[1,512]{1,0:T(1,128)}, bf16[128,128]{1,0:T(8,128)(2,1)}) custom-call(bf16[128,512]{1,0:T(8,128)(2,1)} %get-tuple-element.12.refs_0_, f32[128,512]{1,0:T(8,128)} %get-tuple-element.13.refs_1_, f32[1,512]{1,0:T(1,128)} %get-tuple-element.14.refs_2_, ...), custom_call_target="tpu_custom_call" | custom-call | tf_op jit(solution)/shard_map/hand_over/pallas_call | solution.py:394

commit v5 on v4

--- a/solution.py
+++ b/solution.py
@@ -7,6 +7,7 @@
 
 MESH = pl.DeviceIdType.MESH
 PARTS = 2
+CUTS = (0, 48, 128)
 VMEM_LIMIT = 57 * 10 ** 6
 BF16 = jnp.bfloat16
 F32 = jnp.float32
@@ -73,7 +74,7 @@
     x, z, k = row // 16, (row // 2) % NZ, row % 2
     h, y = col // NZ, col % NZ
     xg, bt = (xg0, xg1), (bt0, bt1)
-    part = [pl.ds(q * (N // PARTS), N // PARTS) for q in range(PARTS)]
+    part = [pl.ds(CUTS[q], CUTS[q + 1] - CUTS[q]) for q in range(PARTS)]
 
     def leaf(x_, z_, k_):
         return (x_ * NZ + z_) * 2 + k_
@@ -132,7 +133,7 @@
     mine = spot(x, z, k)
     scaled = (feat[...].astype(F32).T * nrow).astype(BF16)
     for q in range(PARTS):
-        xg[q][mine] = scaled[q * (N // PARTS):(q + 1) * (N // PARTS)]
+        xg[q][mine] = scaled[CUTS[q]:CUTS[q + 1]]
     pl.semaphore_wait(barrier, len(partners))
 
     for q in range(PARTS):
@@ -182,7 +183,7 @@
                 ps[p, part[q]] = total
             return total
 
-        lax.fori_loop(0, K // 8, forward_turn, jnp.zeros((N // PARTS, N), F32))
+        lax.fori_loop(0, K // 8, forward_turn, jnp.zeros((CUTS[q + 1] - CUTS[q], N), F32))
         for d in FAR + (0,):
             xs2[d, part[q]] = row_sum((1 - h) * NZ + (y + d) % NZ, q).astype(BF16)
             send(2, xs2.at[d, part[q]], xr2.at[d, part[q]], s2x.at[q, d], r2x.at[q, d], xh)
@@ -222,7 +223,7 @@
     projected = lax.dot_general(w[...], dpre[...], (((1,), (1,)), ((), ())), preferred_element_type=F32)
     back_in = (projected * nrow).astype(BF16)
     for q in range(PARTS):
-        bt[q][col] = back_in[q * (N // PARTS):(q + 1) * (N // PARTS)]
+        bt[q][col] = back_in[CUTS[q]:CUTS[q + 1]]
 
     for q in range(PARTS):
         at = bt[q].at[col]
@@ -281,7 +282,7 @@
                 ps[p, part[q]] = total
             return total
 
-        lax.fori_loop(0, K // 8, back_turn, jnp.zeros((N // PARTS, N), F32))
+        lax.fori_loop(0, K // 8, back_turn, jnp.zeros((CUTS[q + 1] - CUTS[q], N), F32))
         for a in (1, 0):
             xa = 1 - x if a else x
             for d in range(NZ):
@@ -357,7 +358,7 @@
     anywhere = pl.BlockSpec(memory_space=pl.ANY)
     sem = pltpu.SemaphoreType.DMA
     tile = lambda *lead: pltpu.VMEM(lead + (N, N), BF16)
-    flat = lambda count: pltpu.VMEM((count, N // PARTS, N), BF16)
+    flat = lambda count: [pltpu.VMEM((count, CUTS[q + 1] - CUTS[q], N), BF16) for q in range(PARTS)]
     wide = lambda kind, *lead: pltpu.VMEM(lead + (WIDE,), kind)
     shapes = (
         jax.ShapeDtypeStruct((N, HID), BF16),
@@ -376,8 +377,8 @@
             pltpu.VMEM((2, K), jnp.int32), pltpu.VMEM((16, N), jnp.int32), pltpu.SMEM((16, N), jnp.int32),
             tile(), pltpu.VMEM((1, N), jnp.int32), pltpu.VMEM((N, HID), BF16), pltpu.VMEM((1, HID), F32),
             pltpu.VMEM((N, HID), BF16),
-            tile(K), flat(32), flat(32), pltpu.VMEM((K, N, N), F32),
-            tile(8), tile(8), tile(8), tile(8), pltpu.VMEM((N, HID), BF16), flat(16), flat(16),
+            tile(K), *flat(32), pltpu.VMEM((K, N, N), F32),
+            tile(8), tile(8), tile(8), tile(8), pltpu.VMEM((N, HID), BF16), *flat(16),
             tile(2, 8), tile(2, 8), tile(8), tile(8), tile(8), tile(8),
             wide(F32, 2, N), wide(F32, 2, 64), wide(F32, 2, 64), wide(BF16, 8, 16), wide(BF16, 8, 16), wide(BF16, 8, 16),
             wide(F32, 4, 16), wide(BF16, 16, 16),

time: 72.4 us -> 71 us (0.981)
  Pallas kernels: 71.6 us -> 70.2 us
    pallas_call x1, Pallas kernels: 69.8 us -> 68.4 us  [shards(): pl.pallas_call(layer, name='layer', out_shape=shapes, in_specs=[anywhere]...]
where the time goes in v5:
time: 71 us; the launch traced here: 70.8 us
  Pallas kernels  70.2 us (99%)
    pallas_call x1, Pallas kernels, shards(): pl.pallas_call(layer, name='layer', out_shape=shapes, in_specs=[anywhere]...  68.4 us
    pallas_call x1, Pallas kernels, shards(): pl.pallas_call(hand_over, name='hand_over', out_shape=shapes, in_specs=[a...  1.8 us

profile of v5, /device:TPU:1, one launch (start us, length us, event | category | flops | bytes accessed | tf_op | source)
XLA Modules:
  0.0 70.8 jit_solution(14641540326100915157)
XLA Ops:
  0.6 68.4 %layer.1 = (bf16[128,512]{1,0:T(8,128)(2,1)}, f32[128,512]{1,0:T(8,128)}, f32[1,512]{1,0:T(1,128)}, bf16[128,128]{1,0:T(8,128)(2,1)}) custom-call(s32[2,32]{1,0:T(2,128)} %bitcast.9, bf16[128,128]{1,0:T(8,128)(2,1)} %feat_hbm.1, s32[1,128]{1,0:T(1,128)} %bitcast.10, bf16[128,512]{1,0:T(8,128)(2,1)} %w_hbm.1, f32[1,512]{1,0:T(1,128)} %bitcast.8, ...), custom_call_target="tpu_custom_call" | custom-call | flops 300000000 | bytes 2000000 | tf_op jit(solution)/shard_map/layer/pallas_call | solution.py:369
  69.0 1.8 %hand_over.1 = (bf16[128,512]{1,0:T(8,128)(2,1)}, f32[128,512]{1,0:T(8,128)}, f32[1,512]{1,0:T(1,128)}, bf16[128,128]{1,0:T(8,128)(2,1)}) custom-call(bf16[128,512]{1,0:T(8,128)(2,1)} %get-tuple-element.12.refs_0_, f32[128,512]{1,0:T(8,128)} %get-tuple-element.13.refs_1_, f32[1,512]{1,0:T(1,128)} %get-tuple-element.14.refs_2_, ...), custom_call_target="tpu_custom_call" | custom-call | tf_op jit(solution)/shard_map/hand_over/pallas_call | solution.py:395

commit v6 on v5

--- a/solution.py
+++ b/solution.py
@@ -328,10 +328,15 @@
             back[q] = back[q] + zr5[d, part[q]].astype(F32)
     gf[...] = (jnp.concatenate(back, axis=0) * nrow).T.astype(BF16)
     stores[1].start()
+
+    def unpack(k_):
+        for i in range(8):
+            rows = pl.ds(pl.multiple_of(k_ * 64 + i // 2 * 16, 16), 16)
+            gw[rows, i % 2 * HID // 2:(i % 2 + 1) * HID // 2] = gwo[k_ * NZ + i, :, :HID // 2].astype(F32)
+
+    unpack(k)
     arrive(gwo.at[pl.ds((1 - k) * NZ, NZ)], sf, rf)
-    for i in range(16):
-        rows, cs = slice(i // 2 * 16, i // 2 * 16 + 16), slice(i % 2 * HID // 2, (i % 2 + 1) * HID // 2)
-        gw[rows, cs] = gwo[i, :, :HID // 2].astype(F32)
+    unpack(1 - k)
     for c in range(HID // N):
         gb[:, c * N:(c + 1) * N] = gwo[c // 2, :, HID // 2:].astype(F32)[c % 2:c % 2 + 1]
     stores[2].start()

time: 71 us -> 71 us (level)
  no operation moved by 1% of the time
where the time goes in v6:
time: 71 us; the launch traced here: 70.8 us
  Pallas kernels  70.2 us (99%)
    pallas_call x1, Pallas kernels, shards(): pl.pallas_call(layer, name='layer', out_shape=shapes, in_specs=[anywhere]...  68.4 us
    pallas_call x1, Pallas kernels, shards(): pl.pallas_call(hand_over, name='hand_over', out_shape=shapes, in_specs=[a...  1.8 us

profile of v6, /device:TPU:1, one launch (start us, length us, event | category | flops | bytes accessed | tf_op | source)
XLA Modules:
  0.0 70.8 jit_solution(13479856164830399579)
XLA Ops:
  0.6 68.4 %layer.1 = (bf16[128,512]{1,0:T(8,128)(2,1)}, f32[128,512]{1,0:T(8,128)}, f32[1,512]{1,0:T(1,128)}, bf16[128,128]{1,0:T(8,128)(2,1)}) custom-call(s32[2,32]{1,0:T(2,128)} %bitcast.9, bf16[128,128]{1,0:T(8,128)(2,1)} %feat_hbm.1, s32[1,128]{1,0:T(1,128)} %bitcast.10, bf16[128,512]{1,0:T(8,128)(2,1)} %w_hbm.1, f32[1,512]{1,0:T(1,128)} %bitcast.8, ...), custom_call_target="tpu_custom_call" | custom-call | flops 300000000 | bytes 2000000 | tf_op jit(solution)/shard_map/layer/pallas_call | solution.py:374
  69.0 1.8 %hand_over.1 = (bf16[128,512]{1,0:T(8,128)(2,1)}, f32[128,512]{1,0:T(8,128)}, f32[1,512]{1,0:T(1,128)}, bf16[128,128]{1,0:T(8,128)(2,1)}) custom-call(bf16[128,512]{1,0:T(8,128)(2,1)} %get-tuple-element.12.refs_0_, f32[128,512]{1,0:T(8,128)} %get-tuple-element.13.refs_1_, f32[1,512]{1,0:T(1,128)} %get-tuple-element.14.refs_2_, ...), custom_call_target="tpu_custom_call" | custom-call | tf_op jit(solution)/shard_map/hand_over/pallas_call | solution.py:400
